TPU v7x, 1024 devices: a whole 4x4x32 slice. The times are simulated.
1024 devices in a mesh: win: 4 (over x), lat: 16 (over z_hi, y, core), lon: 16 (over z_lo).
Axes of the slice: x: 4, y: 4, z: 32 (z_hi: 2, z_lo: 16; z = z_hi * 16 + z_lo), core: 2. Of those that a mesh axis runs over, the one named last changes fastest.
Arguments:
- increment: float32 [4, 3, 1024, 4096], P('win', None, 'lat', 'lon'), may hold values from -6 to 6
- model_weight: float32 [4, 3, 1024, 4096], P('win', None, 'lat', 'lon'), may hold values from 0.25 to 4
- winds: float32 [4, 2, 1024, 4096], P('win', None, 'lat', 'lon'), may hold values from -0.3 to 0.3
- reaction: float32 [4, 3, 3], P('win'), may hold values from -1 to 1
- obs_cells: int32 [4, 16, 16, 1024], P('win', 'lat', 'lon'), may hold values from 0 to 16383
- obs_weight: float32 [4, 3, 16, 16, 1024], P('win', None, 'lat', 'lon'), may hold values from 0.5 to 8
Outputs:
- hess_vec: float32 [4, 3, 1024, 4096], P('win', None, 'lat', 'lon')
Inputs may be any that keep to these rules, and one draw needn't show every extreme that they name: `obs_cells`: an index row * 256 + column within its tile.
All inputs are finite; a program needn't handle non-finite values.
Results may differ from a plain program's by a relative error of at most 0.00002.
Values sent between devices are 32-bit elements; how exact they have to be, the bound alone decides.
A program may use at most 64 MiB of HBM per device.

v0:
```python
import jax
import jax.numpy as jnp
from jax import lax
from jax.sharding import PartitionSpec as P

DIFFUSION = 0.15


def from_behind(value, axis, steps):
    count = lax.axis_size(axis)
    first, last = (max(0, -steps), min(count, count - steps))
    return lax.ppermute(value, axis, [(source, source + steps) for source in range(first, last)])


def extended_2(block, sides, width):
    for axis, dim in sides:
        count = lax.axis_size(axis)
        forward = [(i, i + 1) for i in range(count - 1)]
        forward.append((count - 1, 0))
        backward = [(target, source) for source, target in forward]
        low = lax.ppermute(
            lax.slice_in_dim(block, block.shape[dim] - width, None, axis=dim), axis, forward
        )
        high = lax.ppermute(lax.slice_in_dim(block, 0, width, axis=dim), axis, backward)
        block = jnp.concatenate([low, block, high], axis=dim)
    return block


def send_ahead(field):
    return from_behind(field, "win", 1)


def send_behind(field):
    return from_behind(field, "win", -1)


def sides(extended):
    center = extended[:, 1:-1, 1:-1]
    north_side = extended[:, 2:, 1:-1]
    south_side = extended[:, :-2, 1:-1]
    east_side = extended[:, 1:-1, 2:]
    west_side = extended[:, 1:-1, :-2]
    return (center, north_side, south_side, east_side, west_side)


def crop_to(array, row_count, column_count):
    row_off = (array.shape[-2] - row_count) // 2
    col_off = (array.shape[-1] - column_count) // 2
    return array[..., row_off : row_off + row_count, col_off : col_off + column_count]


def mixing(reaction, field):
    return jnp.sum(reaction[:, :, None, None] * field[None], axis=1)


def per_device(increment, model_weight, winds, reaction, obs_cells, obs_weight):
    field = increment[0]
    weight = model_weight[0]
    wind_now = winds[0]
    mixer = reaction[0]
    cells = obs_cells[0, 0, 0]
    obs_scale = obs_weight[0, :, 0, 0]
    count_fields = field.shape[0]
    rows_here = field.shape[1]
    lat_start = lax.axis_index("lat") * rows_here
    lat_total = rows_here * lax.axis_size("lat")
    depth = 1

    def clear_rims(extended):
        margin = (extended.shape[1] - rows_here) // 2
        if margin == 0:
            return extended
        global_rows = lat_start - margin + jnp.arange(extended.shape[1], dtype=jnp.int32)
        inside = (global_rows >= 0) & (global_rows < lat_total)
        return jnp.where(inside[None, :, None], extended, 0.0)

    def extend_single(state):
        return clear_rims(extended_2(state, (("lat", 1), ("lon", 2)), 1))

    wind_ext = clear_rims(extended_2(wind_now, (("lat", 1), ("lon", 2)), depth))

    def tangent_core(extended):
        center, north_side, south_side, east_side, west_side = sides(extended)
        wind_here = crop_to(wind_ext, center.shape[1], center.shape[2])
        spread = north_side + south_side + east_side + west_side
        result = (1.0 - 4.0 * DIFFUSION) * center + DIFFUSION * spread
        result = (
            result
            - wind_here[0] * (east_side - west_side)
            - wind_here[1] * (north_side - south_side)
        )
        return clear_rims(result + mixing(mixer, center))

    def adjoint_core(extended):
        center, north_side, south_side, east_side, west_side = sides(extended)
        wind_here = crop_to(wind_ext, extended.shape[1], extended.shape[2])
        spread = north_side + south_side + east_side + west_side
        lon_flux = sides(wind_here[0][None] * extended)
        lat_flux = sides(wind_here[1][None] * extended)
        result = (1.0 - 4.0 * DIFFUSION) * center + DIFFUSION * spread
        result = result + (lon_flux[3] - lon_flux[4]) + (lat_flux[1] - lat_flux[2])
        return clear_rims(result + mixing(mixer.T, center))

    forward = tangent_core(extend_single(tangent_core(extend_single(field))))
    flat = forward.reshape(count_fields, -1)
    picked = jnp.take(flat, cells, axis=1)
    placed = jnp.zeros_like(flat).at[:, cells].add(obs_scale * picked)
    observed = placed.reshape(forward.shape)
    earlier = send_ahead(forward)
    jump = weight * (field - earlier)
    later = send_behind(jump)
    back = adjoint_core(extend_single(adjoint_core(extend_single(observed - later))))
    return (jump + back)[None]


def solution(mesh):
    in_specs = (
        P("win", None, "lat", "lon"),
        P("win", None, "lat", "lon"),
        P("win", None, "lat", "lon"),
        P("win", None, None),
        P("win", "lat", "lon", None),
        P("win", None, "lat", "lon", None),
    )
    out_specs = P("win", None, "lat", "lon")
    return jax.shard_map(
        per_device, mesh=mesh, in_specs=in_specs, out_specs=out_specs, check_vma=False
    )
```

profile of v0, /device:TPU:31, one launch (start us, length us, event | category | flops | bytes accessed | tf_op | source)
XLA Modules:
  0.0 330.1 jit_solution(16925988015285087106)
XLA Ops:
  0.0 0.8 fusion.29
  0.8 28.9 %collective-permute-start.4 = (f32[2,1,256]{2,1,0:T(1,128)S(1)}, f32[2,1,256]{2,1,0:T(1,128)S(1)}, u32[]{:S(2)}, u32[]{:S(2)}) collective-permute-start(f32[2,1,256]{2,1,0:T(1,128)S(1)} %get-tuple-element.31), channel_id=1, source_target_pairs={{0,16},{16,32},{32,48},{48,64},{64,80},{80,96},{96,112},{112,128},... | collective-permute-start | bytes 6152 | tf_op jit(solution)/shard_map/ppermute | solution.py:21
  29.7 1.9 collective-permute-start.5
  31.7 0.8 fusion.27
  32.4 24.1 %collective-permute-start = (f32[3,1,256]{2,1,0:T(1,128)S(1)}, f32[3,1,256]{2,1,0:T(1,128)S(1)}, u32[]{:S(2)}, u32[]{:S(2)}) collective-permute-start(f32[3,1,256]{2,1,0:T(1,128)S(1)} %get-tuple-element.27), channel_id=1, source_target_pairs={{0,16},{16,32},{32,48},{48,64},{64,80},{80,96},{96,112},{112,128},... | collective-permute-start | bytes 9224 | tf_op jit(solution)/shard_map/ppermute | solution.py:21
  56.5 1.9 collective-permute-start.1
  58.4 0.9 pad_maximum_fusion.4
  59.5 2.6 collective-permute-start.6
  62.1 18.9 %collective-permute-start.7 = (f32[2,66,1]{2,1,0:T(8,128)S(1)}, f32[2,66,1]{2,1,0:T(8,128)S(1)}, u32[]{:S(2)}, u32[]{:S(2)}) collective-permute-start(f32[2,66,1]{2,1,0:T(8,128)S(1)} %get-tuple-element.30), channel_id=1, source_target_pairs={{1,0},{2,1},{3,2},{4,3},{5,4},{6,5},{7,6},{8,7},{9,8},{10,9},{11,1... | collective-permute-start | bytes 1592 | tf_op jit(solution)/shard_map/ppermute | solution.py:24
  81.0 0.7 copy.22
  81.7 0.7 collective-permute-done.7
  82.4 1.1 maximum_select_fusion.4
  83.5 1.0 pad_maximum_fusion
  84.5 1.9 collective-permute-start.2
  86.4 20.0 %collective-permute-start.3 = (f32[3,66,1]{2,1,0:T(8,128)S(1)}, f32[3,66,1]{2,1,0:T(8,128)S(1)}, u32[]{:S(2)}, u32[]{:S(2)}) collective-permute-start(f32[3,66,1]{2,1,0:T(8,128)S(1)} %get-tuple-element.20), channel_id=1, source_target_pairs={{1,0},{2,1},{3,2},{4,3},{5,4},{6,5},{7,6},{8,7},{9,8},{10,9},{11,1... | collective-permute-start | bytes 2384 | tf_op jit(solution)/shard_map/ppermute | solution.py:24
  106.4 0.1 slice_bitcast_fusion.3
  106.5 0.1 collective-permute-done.2
  106.6 1.5 collective-permute-done.3
  108.1 1.1 maximum_select_fusion
  109.3 0.1 slice.222
  109.4 0.1 multiply_reduce_fusion.3
  109.5 0.3 subtract_add_fusion.1
  109.8 26.4 %collective-permute-start.8 = (f32[3,1,256]{2,1,0:T(1,128)S(1)}, f32[3,1,256]{2,1,0:T(1,128)S(1)}, u32[]{:S(2)}, u32[]{:S(2)}) collective-permute-start(f32[3,1,256]{2,1,0:T(1,128)S(1)} %get-tuple-element.25), channel_id=1, source_target_pairs={{0,16},{16,32},{32,48},{48,64},{64,80},{80,96},{96,112},{112,128},... | collective-permute-start | bytes 9224 | tf_op jit(solution)/shard_map/ppermute | solution.py:21
  136.2 1.9 collective-permute-start.9
  138.1 23.4 %collective-permute-done.9 = f32[3,1,256]{2,1,0:T(1,128)S(1)} collective-permute-done((f32[3,1,256]{2,1,0:T(1,128)S(1)}, f32[3,1,256]{2,1,0:T(1,128)S(1)}, u32[]{:S(2)}, u32[]{:S(2)}) %collective-permute-start.9) | collective-permute-done | bytes 3104 | tf_op jit(solution)/shard_map/ppermute | solution.py:24
  161.7 1.9 collective-permute-start.10
  163.6 20.4 %collective-permute-start.11 = (f32[3,66,1]{2,1,0:T(8,128)S(1)}, f32[3,66,1]{2,1,0:T(8,128)S(1)}, u32[]{:S(2)}, u32[]{:S(2)}) collective-permute-start(f32[3,66,1]{2,1,0:T(8,128)S(1)} %get-tuple-element.16), channel_id=1, source_target_pairs={{1,0},{2,1},{3,2},{4,3},{5,4},{6,5},{7,6},{8,7},{9,8},{10,9},{11,1... | collective-permute-start | bytes 2384 | tf_op jit(solution)/shard_map/ppermute | solution.py:24
  184.0 0.7 compare_select_fusion
  184.7 0.9 copy.15
  185.7 0.1 collective-permute-done.11
  185.8 0.2 maximum_select_fusion.1
  186.0 0.1 slice.237
  186.1 0.1 multiply_reduce_fusion.2
  186.2 0.3 subtract_add_fusion
  186.5 1.3 collective-permute-start.12
  187.8 5.1 %collective-permute-done.12 = f32[3,64,256]{2,1,0:T(8,128)S(1)} collective-permute-done((f32[3,64,256]{2,1,0:T(8,128)S(1)}, f32[3,64,256]{2,1,0:T(8,128)S(1)}, u32[]{:S(2)}, u32[]{:S(2)}) %collective-permute-start.12) | collective-permute-done | bytes 196640 | tf_op jit(solution)/shard_map/ppermute | solution.py:12
  193.0 2.5 collective-permute-start.13
  195.5 4.7 %copy.16 = f32[3,64,256]{0,2,1:T(8,128)} copy(f32[3,64,256]{2,1,0:T(8,128)S(1)} %subtract_add_fusion) | data formatting | bytes 393216 | tf_op jit(solution)/shard_map/add | solution.py:92
  200.1 16.1 %scatter_custom_fusion = f32[3,16384]{0,1:T(8,128)} fusion(s32[1024]{0:T(1024)S(1)} %bitcast.54, f32[]{:T(128)} %constant.10.clone.1, f32[1,3,1,1,1024]{1,4,3,2,0:T(8,128)S(1)} %copy.15, f32[]{:T(128)} %constant.37.clone.1, pred[1024]{0:T(1024)(128)(4,1)S(1)} %compare_and_fusion, f32[3,16384]{0,1:T(8,128)} %bitcast.40, s32[1024]{0:T(1024)S(1)} %broadcast_clamp_fusion), kind=kCustom, calls=%fused_computation.2 | custom fusion | flops 9216 | bytes 922632 | tf_op jit(solution)/shard_map/scatter-add | solution.py:107
  216.2 5.2 %copy.17 = f32[3,64,256]{2,1,0:T(8,128)S(1)} copy(f32[3,64,256]{0,2,1:T(8,128)} %bitcast.41) | data formatting | bytes 393216 | tf_op jit(solution)/shard_map/reshape | solution.py:108
  221.5 4.2 %collective-permute-start.14 = (f32[3,1,256]{2,1,0:T(1,128)S(1)}, f32[3,1,256]{2,1,0:T(1,128)S(1)}, u32[]{:S(2)}, u32[]{:S(2)}) collective-permute-start(f32[3,1,256]{2,1,0:T(1,128)S(1)} %get-tuple-element.23), channel_id=1, source_target_pairs={{0,16},{16,32},{32,48},{48,64},{64,80},{80,96},{96,112},{112,128},... | collective-permute-start | bytes 9224 | tf_op jit(solution)/shard_map/ppermute | solution.py:21
  225.8 1.9 collective-permute-start.15
  227.7 0.1 copy.20
  227.8 23.3 %collective-permute-done.15 = f32[3,1,256]{2,1,0:T(1,128)S(1)} collective-permute-done((f32[3,1,256]{2,1,0:T(1,128)S(1)}, f32[3,1,256]{2,1,0:T(1,128)S(1)}, u32[]{:S(2)}, u32[]{:S(2)}) %collective-permute-start.15) | collective-permute-done | bytes 3104 | tf_op jit(solution)/shard_map/ppermute | solution.py:24
  251.1 0.1 fusion.21
  251.2 1.9 collective-permute-start.16
  253.2 20.4 %collective-permute-start.17 = (f32[3,66,1]{2,1,0:T(8,128)S(1)}, f32[3,66,1]{2,1,0:T(8,128)S(1)}, u32[]{:S(2)}, u32[]{:S(2)}) collective-permute-start(f32[3,66,1]{2,1,0:T(8,128)S(1)} %get-tuple-element.14), channel_id=1, source_target_pairs={{1,0},{2,1},{3,2},{4,3},{5,4},{6,5},{7,6},{8,7},{9,8},{10,9},{11,1... | collective-permute-start | bytes 2384 | tf_op jit(solution)/shard_map/ppermute | solution.py:24
  273.6 0.3 collective-permute-done.16
  274.0 1.4 collective-permute-done.17
  275.3 0.2 broadcast_multiply_fusion.3
  275.6 0.1 slice.246
  275.7 0.1 multiply_reduce_fusion.1
  275.8 0.4 fusion.15
  276.3 2.8 collective-permute-start.18
  279.1 1.9 collective-permute-start.19
  281.0 23.4 %collective-permute-done.19 = f32[3,1,256]{2,1,0:T(1,128)S(1)} collective-permute-done((f32[3,1,256]{2,1,0:T(1,128)S(1)}, f32[3,1,256]{2,1,0:T(1,128)S(1)}, u32[]{:S(2)}, u32[]{:S(2)}) %collective-permute-start.19) | collective-permute-done | bytes 3104 | tf_op jit(solution)/shard_map/ppermute | solution.py:24
  304.6 1.9 collective-permute-start.20
  306.5 20.3 %collective-permute-start.21 = (f32[3,66,1]{2,1,0:T(8,128)S(1)}, f32[3,66,1]{2,1,0:T(8,128)S(1)}, u32[]{:S(2)}, u32[]{:S(2)}) collective-permute-start(f32[3,66,1]{2,1,0:T(8,128)S(1)} %get-tuple-element.10), channel_id=1, source_target_pairs={{1,0},{2,1},{3,2},{4,3},{5,4},{6,5},{7,6},{8,7},{9,8},{10,9},{11,1... | collective-permute-start | bytes 2384 | tf_op jit(solution)/shard_map/ppermute | solution.py:24
  326.8 0.2 collective-permute-done.20
  327.0 1.5 collective-permute-done.21
  328.5 0.2 broadcast_multiply_fusion.2
  328.8 0.1 slice.261
  328.9 0.1 multiply_reduce_fusion
  329.0 1.1 fusion.10
  (36 shorter events, 0.7 us)
Async XLA Ops:
  0.0 192.9 %copy-start = (f32[1,3,64,256]{3,2,1,0:T(8,128)S(1)}, f32[1,3,64,256]{3,2,1,0:T(8,128)}, u32[]{:S(2)}) copy-start(f32[1,3,64,256]{3,2,1,0:T(8,128)} %param.6) | copy-start | bytes 589828
  0.0 195.4 %copy-start.2 = (s32[1,1,1,1024]{3,2,1,0:T(1,128)S(1)}, s32[1,1,1,1024]{3,2,1,0:T(1,128)}, u32[]{:S(2)}) copy-start(s32[1,1,1,1024]{3,2,1,0:T(1,128)} %param.10) | copy-start | bytes 12292
  0.0 192.9 %copy-start.1 = (f32[1,3,64,256]{3,2,1,0:T(8,128)S(1)}, f32[1,3,64,256]{3,2,1,0:T(8,128)}, u32[]{:S(2)}) copy-start(f32[1,3,64,256]{3,2,1,0:T(8,128)} %param.7) | copy-start | bytes 589828
  0.8 57.6 %collective-permute-start.4 = (f32[2,1,256]{2,1,0:T(1,128)S(1)}, f32[2,1,256]{2,1,0:T(1,128)S(1)}, u32[]{:S(2)}, u32[]{:S(2)}) collective-permute-start(f32[2,1,256]{2,1,0:T(1,128)S(1)} %get-tuple-element.31), channel_id=1, source_target_pairs={{0,16},{16,32},{32,48},{48,64},{64,80},{80,96},{96,112},{112,128},... | collective-permute-start | bytes 6152 | tf_op jit(solution)/shard_map/ppermute | solution.py:21
  29.7 28.7 %collective-permute-start.5 = (f32[2,1,256]{2,1,0:T(1,128)S(1)}, f32[2,1,256]{2,1,0:T(1,128)S(1)}, u32[]{:S(2)}, u32[]{:S(2)}) collective-permute-start(f32[2,1,256]{2,1,0:T(1,128)S(1)} %get-tuple-element.32), channel_id=1, source_target_pairs={{16,0},{32,16},{48,32},{64,48},{80,64},{96,80},{112,96},{128,112},... | collective-permute-start | bytes 6152 | tf_op jit(solution)/shard_map/ppermute | solution.py:24
  32.4 51.0 %collective-permute-start = (f32[3,1,256]{2,1,0:T(1,128)S(1)}, f32[3,1,256]{2,1,0:T(1,128)S(1)}, u32[]{:S(2)}, u32[]{:S(2)}) collective-permute-start(f32[3,1,256]{2,1,0:T(1,128)S(1)} %get-tuple-element.27), channel_id=1, source_target_pairs={{0,16},{16,32},{32,48},{48,64},{64,80},{80,96},{96,112},{112,128},... | collective-permute-start | bytes 9224 | tf_op jit(solution)/shard_map/ppermute | solution.py:21
  56.5 27.0 %collective-permute-start.1 = (f32[3,1,256]{2,1,0:T(1,128)S(1)}, f32[3,1,256]{2,1,0:T(1,128)S(1)}, u32[]{:S(2)}, u32[]{:S(2)}) collective-permute-start(f32[3,1,256]{2,1,0:T(1,128)S(1)} %get-tuple-element.28), channel_id=1, source_target_pairs={{16,0},{32,16},{48,32},{64,48},{80,64},{96,80},{112,96},{128,112},... | collective-permute-start | bytes 9224 | tf_op jit(solution)/shard_map/ppermute | solution.py:24
  59.5 22.2 %collective-permute-start.6 = (f32[2,66,1]{2,1,0:T(8,128)S(1)}, f32[2,66,1]{2,1,0:T(8,128)S(1)}, u32[]{:S(2)}, u32[]{:S(2)}) collective-permute-start(f32[2,66,1]{2,1,0:T(8,128)S(1)} %get-tuple-element.29), channel_id=1, source_target_pairs={{0,1},{1,2},{2,3},{3,4},{4,5},{5,6},{6,7},{7,8},{8,9},{9,10},{10,1... | collective-permute-start | bytes 1592 | tf_op jit(solution)/shard_map/ppermute | solution.py:21
  62.1 20.2 %collective-permute-start.7 = (f32[2,66,1]{2,1,0:T(8,128)S(1)}, f32[2,66,1]{2,1,0:T(8,128)S(1)}, u32[]{:S(2)}, u32[]{:S(2)}) collective-permute-start(f32[2,66,1]{2,1,0:T(8,128)S(1)} %get-tuple-element.30), channel_id=1, source_target_pairs={{1,0},{2,1},{3,2},{4,3},{5,4},{6,5},{7,6},{8,7},{9,8},{10,9},{11,1... | collective-permute-start | bytes 1592 | tf_op jit(solution)/shard_map/ppermute | solution.py:24
  84.5 22.1 %collective-permute-start.2 = (f32[3,66,1]{2,1,0:T(8,128)S(1)}, f32[3,66,1]{2,1,0:T(8,128)S(1)}, u32[]{:S(2)}, u32[]{:S(2)}) collective-permute-start(f32[3,66,1]{2,1,0:T(8,128)S(1)} %get-tuple-element.19), channel_id=1, source_target_pairs={{0,1},{1,2},{2,3},{3,4},{4,5},{5,6},{6,7},{7,8},{8,9},{9,10},{10,1... | collective-permute-start | bytes 2384 | tf_op jit(solution)/shard_map/ppermute | solution.py:21
  86.4 21.7 %collective-permute-start.3 = (f32[3,66,1]{2,1,0:T(8,128)S(1)}, f32[3,66,1]{2,1,0:T(8,128)S(1)}, u32[]{:S(2)}, u32[]{:S(2)}) collective-permute-start(f32[3,66,1]{2,1,0:T(8,128)S(1)} %get-tuple-element.20), channel_id=1, source_target_pairs={{1,0},{2,1},{3,2},{4,3},{5,4},{6,5},{7,6},{8,7},{9,8},{10,9},{11,1... | collective-permute-start | bytes 2384 | tf_op jit(solution)/shard_map/ppermute | solution.py:24
  109.8 28.3 %collective-permute-start.8 = (f32[3,1,256]{2,1,0:T(1,128)S(1)}, f32[3,1,256]{2,1,0:T(1,128)S(1)}, u32[]{:S(2)}, u32[]{:S(2)}) collective-permute-start(f32[3,1,256]{2,1,0:T(1,128)S(1)} %get-tuple-element.25), channel_id=1, source_target_pairs={{0,16},{16,32},{32,48},{48,64},{64,80},{80,96},{96,112},{112,128},... | collective-permute-start | bytes 9224 | tf_op jit(solution)/shard_map/ppermute | solution.py:21
  136.2 25.4 %collective-permute-start.9 = (f32[3,1,256]{2,1,0:T(1,128)S(1)}, f32[3,1,256]{2,1,0:T(1,128)S(1)}, u32[]{:S(2)}, u32[]{:S(2)}) collective-permute-start(f32[3,1,256]{2,1,0:T(1,128)S(1)} %get-tuple-element.26), channel_id=1, source_target_pairs={{16,0},{32,16},{48,32},{64,48},{80,64},{96,80},{112,96},{128,112},... | collective-permute-start | bytes 9224 | tf_op jit(solution)/shard_map/ppermute | solution.py:24
  161.7 24.0 %collective-permute-start.10 = (f32[3,66,1]{2,1,0:T(8,128)S(1)}, f32[3,66,1]{2,1,0:T(8,128)S(1)}, u32[]{:S(2)}, u32[]{:S(2)}) collective-permute-start(f32[3,66,1]{2,1,0:T(8,128)S(1)} %get-tuple-element.15), channel_id=1, source_target_pairs={{0,1},{1,2},{2,3},{3,4},{4,5},{5,6},{6,7},{7,8},{8,9},{9,10},{10,1... | collective-permute-start | bytes 2384 | tf_op jit(solution)/shard_map/ppermute | solution.py:21
  163.6 22.2 %collective-permute-start.11 = (f32[3,66,1]{2,1,0:T(8,128)S(1)}, f32[3,66,1]{2,1,0:T(8,128)S(1)}, u32[]{:S(2)}, u32[]{:S(2)}) collective-permute-start(f32[3,66,1]{2,1,0:T(8,128)S(1)} %get-tuple-element.16), channel_id=1, source_target_pairs={{1,0},{2,1},{3,2},{4,3},{5,4},{6,5},{7,6},{8,7},{9,8},{10,9},{11,1... | collective-permute-start | bytes 2384 | tf_op jit(solution)/shard_map/ppermute | solution.py:24
  186.5 6.4 %collective-permute-start.12 = (f32[3,64,256]{2,1,0:T(8,128)S(1)}, f32[3,64,256]{2,1,0:T(8,128)S(1)}, u32[]{:S(2)}, u32[]{:S(2)}) collective-permute-start(f32[3,64,256]{2,1,0:T(8,128)S(1)} %subtract_add_fusion), channel_id=1, source_target_pairs={{0,256},{256,512},{512,768},{1,257},{257,513},{513,769},{2,258},{2... | collective-permute-start | bytes 589832 | tf_op jit(solution)/shard_map/ppermute | solution.py:12
  193.0 28.5 %collective-permute-start.13 = (f32[3,64,256]{2,1,0:T(8,128)S(1)}, f32[3,64,256]{2,1,0:T(8,128)S(1)}, u32[]{:S(2)}, u32[]{:S(2)}) collective-permute-start(f32[3,64,256]{2,1,0:T(8,128)S(1)} %bitcast_multiply_fusion.2), channel_id=1, source_target_pairs={{256,0},{512,256},{768,512},{257,1},{513,257},{769,513},{258,2},{5... | collective-permute-start | bytes 589832 | tf_op jit(solution)/shard_map/ppermute | solution.py:12
  216.2 11.5 %copy-start.3 = (f32[1,3,3]{2,0,1:T(1,128)S(1)}, f32[1,3,3]{2,0,1:T(1,128)}, u32[]{:S(2)}) copy-start(f32[1,3,3]{2,0,1:T(1,128)} %param.9) | copy-start | bytes 112
  221.5 6.3 %collective-permute-start.14 = (f32[3,1,256]{2,1,0:T(1,128)S(1)}, f32[3,1,256]{2,1,0:T(1,128)S(1)}, u32[]{:S(2)}, u32[]{:S(2)}) collective-permute-start(f32[3,1,256]{2,1,0:T(1,128)S(1)} %get-tuple-element.23), channel_id=1, source_target_pairs={{0,16},{16,32},{32,48},{48,64},{64,80},{80,96},{96,112},{112,128},... | collective-permute-start | bytes 9224 | tf_op jit(solution)/shard_map/ppermute | solution.py:21
  225.8 25.4 %collective-permute-start.15 = (f32[3,1,256]{2,1,0:T(1,128)S(1)}, f32[3,1,256]{2,1,0:T(1,128)S(1)}, u32[]{:S(2)}, u32[]{:S(2)}) collective-permute-start(f32[3,1,256]{2,1,0:T(1,128)S(1)} %get-tuple-element.24), channel_id=1, source_target_pairs={{16,0},{32,16},{48,32},{64,48},{80,64},{96,80},{112,96},{128,112},... | collective-permute-start | bytes 9224 | tf_op jit(solution)/shard_map/ppermute | solution.py:24
  251.2 22.7 %collective-permute-start.16 = (f32[3,66,1]{2,1,0:T(8,128)S(1)}, f32[3,66,1]{2,1,0:T(8,128)S(1)}, u32[]{:S(2)}, u32[]{:S(2)}) collective-permute-start(f32[3,66,1]{2,1,0:T(8,128)S(1)} %get-tuple-element.13), channel_id=1, source_target_pairs={{0,1},{1,2},{2,3},{3,4},{4,5},{5,6},{6,7},{7,8},{8,9},{9,10},{10,1... | collective-permute-start | bytes 2384 | tf_op jit(solution)/shard_map/ppermute | solution.py:21
  253.2 22.2 %collective-permute-start.17 = (f32[3,66,1]{2,1,0:T(8,128)S(1)}, f32[3,66,1]{2,1,0:T(8,128)S(1)}, u32[]{:S(2)}, u32[]{:S(2)}) collective-permute-start(f32[3,66,1]{2,1,0:T(8,128)S(1)} %get-tuple-element.14), channel_id=1, source_target_pairs={{1,0},{2,1},{3,2},{4,3},{5,4},{6,5},{7,6},{8,7},{9,8},{10,9},{11,1... | collective-permute-start | bytes 2384 | tf_op jit(solution)/shard_map/ppermute | solution.py:24
  276.3 4.7 %collective-permute-start.18 = (f32[3,1,256]{2,1,0:T(1,128)S(1)}, f32[3,1,256]{2,1,0:T(1,128)S(1)}, u32[]{:S(2)}, u32[]{:S(2)}) collective-permute-start(f32[3,1,256]{2,1,0:T(1,128)S(1)} %get-tuple-element.21), channel_id=1, source_target_pairs={{0,16},{16,32},{32,48},{48,64},{64,80},{80,96},{96,112},{112,128},... | collective-permute-start | bytes 9224 | tf_op jit(solution)/shard_map/ppermute | solution.py:21
  279.1 25.4 %collective-permute-start.19 = (f32[3,1,256]{2,1,0:T(1,128)S(1)}, f32[3,1,256]{2,1,0:T(1,128)S(1)}, u32[]{:S(2)}, u32[]{:S(2)}) collective-permute-start(f32[3,1,256]{2,1,0:T(1,128)S(1)} %get-tuple-element.22), channel_id=1, source_target_pairs={{16,0},{32,16},{48,32},{64,48},{80,64},{96,80},{112,96},{128,112},... | collective-permute-start | bytes 9224 | tf_op jit(solution)/shard_map/ppermute | solution.py:24
  304.6 22.4 %collective-permute-start.20 = (f32[3,66,1]{2,1,0:T(8,128)S(1)}, f32[3,66,1]{2,1,0:T(8,128)S(1)}, u32[]{:S(2)}, u32[]{:S(2)}) collective-permute-start(f32[3,66,1]{2,1,0:T(8,128)S(1)} %get-tuple-element.9), channel_id=1, source_target_pairs={{0,1},{1,2},{2,3},{3,4},{4,5},{5,6},{6,7},{7,8},{8,9},{9,10},{10,1... | collective-permute-start | bytes 2384 | tf_op jit(solution)/shard_map/ppermute | solution.py:21
  306.5 22.0 %collective-permute-start.21 = (f32[3,66,1]{2,1,0:T(8,128)S(1)}, f32[3,66,1]{2,1,0:T(8,128)S(1)}, u32[]{:S(2)}, u32[]{:S(2)}) collective-permute-start(f32[3,66,1]{2,1,0:T(8,128)S(1)} %get-tuple-element.10), channel_id=1, source_target_pairs={{1,0},{2,1},{3,2},{4,3},{5,4},{6,5},{7,6},{8,7},{9,8},{10,9},{11,1... | collective-permute-start | bytes 2384 | tf_op jit(solution)/shard_map/ppermute | solution.py:24
where the time goes:
time: 331 us; the launch traced here: 330 us
  starting transfers between devices  210 us (63%)
  waiting for transfers between devices  81.1 us (25%)
  other arithmetic  24.3 us (7%)
  local copies, waits for them, and re-layouts  14.2 us (4%)
    ppermute x10, starting transfers between devices, extended_2(): lax.ppermute(lax.slice_in_dim(block, 0, width, axis=dim), axis, backward)  110 us
    ppermute x10, starting transfers between devices, extended_2(): lax.ppermute(lax.slice_in_dim(block, block.shape[dim] - width, None, axis...  96.7 us
    ppermute x10, waiting for transfers between devices, extended_2(): lax.ppermute(lax.slice_in_dim(block, 0, width, axis=dim), axis, backward)  75.4 us
    scatter-add x1, other arithmetic, per_device(): placed = jnp.zeros_like(flat).at[:, cells].add(obs_scale * picked)  16.1 us
  transfers between devices with their start and end apart: 22, of which 12 were waited for; matrix products, arithmetic and copies ran while one was open for 10% of the time, Pallas kernels for 0%

commit v1 on v0

v1 whole, which is shorter than its diff:
```python
import functools

import jax
import jax.numpy as jnp
from jax import lax
from jax.experimental import pallas as pl
from jax.experimental.pallas import tpu as pltpu
from jax.sharding import PartitionSpec as P

DIFFUSION = 0.15
KEEP = 1.0 - 4.0 * DIFFUSION
MESH = pl.DeviceIdType.MESH
F32 = jnp.float32
BF16 = jnp.bfloat16
DIRS = ((1, 0), (-1, 0), (0, 1), (0, -1), (1, 1), (1, -1), (-1, 1), (-1, -1))


def rolled(x, shift, axis):
    shift = shift % x.shape[axis]
    return x if shift == 0 else pltpu.roll(x, shift, axis)


def east(x):
    return rolled(x, -1, 1)


def west(x):
    return rolled(x, 1, 1)


def north(x):
    return rolled(x, -1, 0)


def south(x):
    return rolled(x, 1, 0)


def tangent(xs, coef, mix):
    a, b, c, d = coef
    out = []
    for f in range(3):
        x = xs[f]
        y = a * east(x) + b * west(x) + c * north(x) + d * south(x)
        out.append(y + mix[f][0] * xs[0] + mix[f][1] * xs[1] + mix[f][2] * xs[2])
    return out


def adjoint(zs, coef, mix):
    a, b, c, d = coef
    out = []
    for f in range(3):
        z = zs[f]
        y = east(b * z) + west(a * z) + north(d * z) + south(c * z)
        out.append(y + mix[0][f] * zs[0] + mix[1][f] * zs[1] + mix[2][f] * zs[2])
    return out


def iota(shape, axis):
    return lax.broadcasted_iota(jnp.int32, shape, axis)


def kernel(
    sizes,
    inc_h, mw_h, winds_h, rea_h, cells_h, ow_h,
    out_ref,
    x_ext, u_ext, w_ext, coef, g_ext, h_ext, t_ext,
    mw_v, rea_s, cells_v, ow_v,
    pack, ce, cw, rows_own, rows_far, fwd0, ring_r, ring_c,
    got_rows_own, got_rows_far, got_cols, got_corner, inc_n, mw_n, got_fwd, got_ring_r, got_ring_c,
    load_sem, send_sem, recv_sem, xsend_sem, xrecv_sem,
):
    n_win, n_lat, n_lon = sizes
    win, lat, lon = lax.axis_index("win"), lax.axis_index("lat"), lax.axis_index("lon")
    R, C = 64, 256

    def lon_at(step):
        return lax.rem(lon + step + n_lon, n_lon)

    def lat_ok(step):
        return (lat + step >= 0) & (lat + step < n_lat)

    has_prev, has_next = win > 0, win < n_win - 1

    barrier = pltpu.get_barrier_semaphore()

    def tell(ok, target):
        @pl.when(ok)
        def _():
            pl.semaphore_signal(barrier, inc=1, device_id=target, device_id_type=MESH)

    for dlat, dlon in DIRS:
        tell(lat_ok(-dlat), (win, lat - dlat, lon_at(-dlon)))
        tell(has_next & lat_ok(-dlat), (win + 1, lat - dlat, lon_at(-dlon)))
    tell(has_next, (win + 1, lat, lon))
    tell(has_prev, (win - 1, lat, lon))

    tile = (slice(None), pl.ds(0, R), pl.ds(0, C))
    loads = [
        pltpu.make_async_copy(cells_h.at[0, 0], cells_v, load_sem.at[0]),
        pltpu.make_async_copy(ow_h.at[0, :, 0], ow_v, load_sem.at[1]),
        pltpu.make_async_copy(inc_h.at[0], x_ext.at[tile], load_sem.at[2]),
        pltpu.make_async_copy(winds_h.at[0], u_ext.at[tile], load_sem.at[3]),
        pltpu.make_async_copy(mw_h.at[0], mw_v, load_sem.at[4]),
        pltpu.make_async_copy(rea_h, rea_s, load_sem.at[5]),
    ]
    for load in loads:
        load.start()

    for d, (dlat, dlon) in enumerate(DIRS):
        for dw in range(2):
            there = lat_ok(-dlat) & (has_next if dw else (win >= 0))

            @pl.when(jnp.logical_not(there))
            def _(d=d, dw=dw, dlat=dlat, dlon=dlon):
                if dlon == 0:
                    ref = got_rows_far.at[d] if dw else got_rows_own.at[d]
                elif dlat == 0:
                    ref = got_cols.at[dw, d - 2]
                else:
                    ref = got_corner.at[dw, d - 4]
                ref[...] = jnp.zeros(ref.shape, F32)

    @pl.when(jnp.logical_not(has_next))
    def _():
        inc_n[...] = jnp.zeros(inc_n.shape, F32)
        mw_n[...] = jnp.zeros(mw_n.shape, F32)

    @pl.when(jnp.logical_not(has_prev))
    def _():
        got_fwd[...] = jnp.zeros(got_fwd.shape, F32)
        got_ring_r[...] = jnp.zeros(got_ring_r.shape, F32)
        got_ring_c[...] = jnp.zeros(got_ring_c.shape, F32)

    loads[0].wait()
    loads[1].wait()
    cells = cells_v[...]
    count = cells.shape[1]
    row_of = lax.shift_right_logical(cells, 8)
    col_of = lax.bitwise_and(cells, 255)
    at_row = iota((R, count), 0) == row_of
    at_col = jnp.where(iota((C, count), 0) == col_of, 1.0, 0.0).astype(BF16)
    for f in range(3):
        rest = ow_v[f]
        total = None
        for _ in range(3):
            part = rest.astype(BF16).astype(F32)
            rest = rest - part
            spread = jnp.where(at_row, part, 0.0).astype(BF16)
            term = lax.dot_general(spread, at_col, (((1,), (1,)), ((), ())), preferred_element_type=F32)
            total = term if total is None else total + term
        w_ext[f, 0:R, 0:C] = total

    for load in loads[2:]:
        load.wait()
    mix = [[rea_s[f, 0, g] + (KEEP if f == g else 0.0) for g in range(3)] for f in range(3)]

    lane = iota((R, 128), 1)
    packed = jnp.zeros((R, 128), F32)
    own = [(x_ext, 0), (x_ext, 1), (x_ext, 2), (u_ext, 0), (u_ext, 1), (w_ext, 0), (w_ext, 1), (w_ext, 2), (mw_v, 0), (mw_v, 1), (mw_v, 2)]
    for a, (ref, f) in enumerate(own):
        ends = jnp.where(lane < 64, ref[f, 0:R, 0:128], ref[f, 0:R, C - 128 : C])
        packed = jnp.where((lane >= 8 * a) & (lane < 8 * a + 8), rolled(ends, 8 * a + 4, 1), packed)
    pack[...] = packed
    half = R // 2
    low_lane = lax.rem(iota((half, 128), 1), 8) < 4
    ce[...] = jnp.where(low_lane, packed[:half], rolled(packed[half:], 4, 1))
    cw[...] = jnp.where(low_lane, rolled(packed[half:], -4, 1), packed[:half])

    sub = iota((8, C), 0)
    lu, lv = u_ext[0, R - 8 : R, 0:C], u_ext[1, R - 8 : R, 0:C]
    fu, fv = u_ext[0, 0:8, 0:C], u_ext[1, 0:8, 0:C]
    for f in range(3):
        wind = jnp.where(sub == 1, rolled(lv, -4 - f, 0), rolled(lu, -5 - f, 0))
        obs = rolled(w_ext[f, R - 8 : R, 0:C], 4, 0)
        rows_own[0, f] = jnp.where(sub >= 4, x_ext[f, R - 8 : R, 0:C], jnp.where(sub >= 2, obs, wind))
        wind = jnp.where(sub == 6, rolled(fu, 6 - f, 0), rolled(fv, 7 - f, 0))
        obs = rolled(w_ext[f, 0:8, 0:C], 4, 0)
        rows_own[1, f] = jnp.where(sub < 4, x_ext[f, 0:8, 0:C], jnp.where(sub < 6, obs, wind))
    for pair in range(2):
        n_rows = n_cols = None
        for f in range(2 * pair, min(3, 2 * pair + 2)):
            base = 4 * (f % 2)
            lx, lm = x_ext[f, R - 8 : R, 0:C], mw_v[f, R - 8 : R, 0:C]
            fx, fm = x_ext[f, 0:8, 0:C], mw_v[f, 0:8, 0:C]
            top = jnp.where(lax.rem(sub, 4) >= 2, rolled(lx, -base, 0), rolled(lm, -base - 2, 0))
            bottom = jnp.where(lax.rem(sub, 4) < 2, rolled(fx, base, 0), rolled(fm, base + 2, 0))
            n_rows = top if n_rows is None else jnp.where(sub < 4, top, n_rows)
            n_cols = bottom if n_cols is None else jnp.where(sub >= 4, bottom, n_cols)
        rows_far[0, pair] = n_rows
        rows_far[1, pair] = n_cols

    uc, vc = u_ext[0, 0:R, 0:C], u_ext[1, 0:R, 0:C]
    coef[0, 0:R, 0:C] = DIFFUSION - uc
    coef[1, 0:R, 0:C] = DIFFUSION + uc
    coef[2, 0:R, 0:C] = DIFFUSION - vc
    coef[3, 0:R, 0:C] = DIFFUSION + vc
    c_tile = [coef[i, 0:R, 0:C] for i in range(4)]
    state = [x_ext[f, 0:R, 0:C] for f in range(3)]
    for _ in range(2):
        state = tangent(state, c_tile, mix)
    for f in range(3):
        fwd0[f] = state[f]

    lats = 1 + lat_ok(1).astype(jnp.int32) + lat_ok(-1).astype(jnp.int32)
    prev, nxt = has_prev.astype(jnp.int32), has_next.astype(jnp.int32)
    pl.semaphore_wait(barrier, 3 * lats * (1 + prev) - 1 + nxt)

    def message(d, dw):
        dlat, dlon = DIRS[d]
        if dlon == 0:
            src, dst = (rows_far.at[d], got_rows_far.at[d]) if dw else (rows_own.at[d], got_rows_own.at[d])
        elif dlat == 0:
            src, dst = (ce if dlon == 1 else cw), got_cols.at[dw, d - 2]
        else:
            src, dst = pack.at[pl.ds(R - 8 if dlat == 1 else 0, 8)], got_corner.at[dw, d - 4]
        return pltpu.make_async_remote_copy(
            src_ref=src,
            dst_ref=dst,
            send_sem=send_sem.at[dw, d],
            recv_sem=recv_sem.at[dw, d],
            device_id=(win - dw, lat + dlat, lon_at(dlon)),
            device_id_type=MESH,
        )

    def across(i, src, dst, step):
        return pltpu.make_async_remote_copy(
            src_ref=src,
            dst_ref=dst,
            send_sem=xsend_sem.at[i],
            recv_sem=xrecv_sem.at[i],
            device_id=(win + step, lat, lon),
            device_id_type=MESH,
        )

    def copies(dw):
        for d, (dlat, _) in enumerate(DIRS):
            yield d, lat_ok(dlat) & (has_prev if dw else (win >= 0)), lat_ok(-dlat) & (has_next if dw else (win >= 0))

    for dw in range(2):
        for d, ok, _ in copies(dw):

            @pl.when(ok)
            def _(d=d, dw=dw):
                message(d, dw).start()

    bulk = [across(0, inc_h.at[0], inc_n, -1), across(1, mw_h.at[0], mw_n, -1)]
    first = across(2, fwd0, got_fwd, 1)
    late = [across(3, ring_r, got_ring_r, 1), across(4, ring_c, got_ring_c, 1)]

    @pl.when(has_next)
    def _():
        first.start()

    @pl.when(has_prev)
    def _():
        bulk[0].start()
        bulk[1].start()

    for dw in range(2):
        for d, _, ok in copies(dw):

            @pl.when(ok)
            def _(d=d, dw=dw):
                message(d, dw).wait_recv()

    corner_low = lax.rem(iota((8, 128), 1), 8) < 4
    corner_sub = iota((8, 128), 0)

    def columns(dw):
        from_west, from_east = got_cols[dw, 0], got_cols[dw, 1]
        upper = jnp.where(low_lane, from_west, from_east)
        lower = jnp.where(low_lane, rolled(from_west, -4, 1), rolled(from_east, 4, 1))
        sw, se, nw, ne = (got_corner[dw, i] for i in range(4))
        rim = jnp.where(corner_sub < 4, jnp.where(corner_low, nw, ne), jnp.where(corner_low, sw, se))
        return jnp.concatenate([upper, lower, rim], axis=0)

    own_cols = columns(0)

    def side(cols, a):
        return rolled(cols, -8 * a - 4, 1)

    E = R + 8
    inside = jnp.where(iota((8, C), 0) < 4, lat_ok(1).astype(F32), lat_ok(-1).astype(F32)) > 0.0
    for f in range(3):
        south_rows, north_rows = got_rows_own[0, f], got_rows_own[1, f]
        x_ext[f, :, C:] = side(own_cols, f)
        x_ext[f, R:E, 0:C] = jnp.where(sub < 4, north_rows, south_rows)
        w_ext[f, :, C:] = side(own_cols, 5 + f)
        w_ext[f, R:E, 0:C] = rolled(jnp.where(sub < 4, south_rows, north_rows), 4, 0)
    for i in range(2):
        rows = jnp.zeros((8, C), F32)
        for t in range(3):
            rows = jnp.where(sub == t, rolled(got_rows_own[1, t], t - 6 - i, 0), rows)
            rows = jnp.where(sub == 5 + t, rolled(got_rows_own[0, t], 5 + t - i, 0), rows)
        coef[2 * i, R:E, 0:C] = jnp.where(inside, DIFFUSION - rows, 0.0)
        coef[2 * i + 1, R:E, 0:C] = jnp.where(inside, DIFFUSION + rows, 0.0)
        cols = side(own_cols, 3 + i)
        less, more = DIFFUSION - cols, DIFFUSION + cols
        coef[2 * i, 0:R, C:] = less[0:R]
        coef[2 * i + 1, 0:R, C:] = more[0:R]
        coef[2 * i, R:E, C:] = jnp.where(inside[:, 0:128], less[R:E], 0.0)
        coef[2 * i + 1, R:E, C:] = jnp.where(inside[:, 0:128], more[R:E], 0.0)

    c_all = [coef[i] for i in range(4)]
    state = tangent([x_ext[f] for f in range(3)], c_all, mix)
    for f in range(3):
        t_ext[f] = state[f]
    state = tangent([t_ext[f] for f in range(3)], c_all, mix)

    ring = jnp.zeros((R, 128), F32)
    for f in range(3):
        t_ext[f] = state[f]
        ring_r[f] = jnp.where(sub < 4, t_ext[f, 0:8, 0:C], t_ext[f, R - 8 : R, 0:C])
        ends = jnp.where(lane < 64, t_ext[f, 0:R, 0:128], t_ext[f, 0:R, C - 128 : C])
        ring = jnp.where((lane >= 8 * f) & (lane < 8 * f + 8), rolled(ends, 8 * f + 4, 1), ring)
    quarter = R // 4
    folded = ring[0:quarter]
    group = iota((quarter, 128), 1)
    for q in range(1, 4):
        folded = jnp.where(group >= 32 * q, rolled(ring[quarter * q : quarter * (q + 1)], 32 * q, 1), folded)
    ring_c[...] = folded

    @pl.when(has_next)
    def _():
        late[0].start()
        late[1].start()

    far_cols = columns(1)

    @pl.when(has_next)
    def _():
        bulk[0].wait_recv()
        bulk[1].wait_recv()

    for f in range(3):
        t, base = f // 2, 4 * (f % 2)
        south_rows, north_rows = got_rows_far[0, t], got_rows_far[1, t]
        inc_rows = jnp.where(sub < 4, rolled(north_rows, -base, 0), rolled(south_rows, base, 0))
        mw_rows = jnp.where(sub < 4, rolled(north_rows, -base - 2, 0), rolled(south_rows, base + 2, 0))
        mw_cols = side(far_cols, 8 + f)
        g_ext[f, 0:R, 0:C] = w_ext[f, 0:R, 0:C] + mw_n[f]
        h_ext[f, 0:R, 0:C] = mw_n[f] * inc_n[f]
        g_ext[f, R:E, 0:C] = w_ext[f, R:E, 0:C] + mw_rows
        h_ext[f, R:E, 0:C] = mw_rows * inc_rows
        g_ext[f, :, C:] = w_ext[f, :, C:] + mw_cols
        h_ext[f, :, C:] = mw_cols * side(far_cols, f)

    state = [g_ext[f] * t_ext[f] - h_ext[f] for f in range(3)]
    state = adjoint(state, c_all, mix)
    for f in range(3):
        h_ext[f] = state[f]
    state = adjoint([h_ext[f] for f in range(3)], c_all, mix)
    for f in range(3):
        h_ext[f] = state[f]

    @pl.when(has_prev)
    def _():
        first.wait_recv()
        late[0].wait_recv()
        late[1].wait_recv()

    folded = got_ring_c[...]
    ring = jnp.concatenate([rolled(folded, -32 * q, 1) for q in range(4)], axis=0)
    for f in range(3):
        rows = got_ring_r[f]
        got_fwd[f, 0:8] = jnp.where(sub < 2, rows, got_fwd[f, 0:8])
        got_fwd[f, R - 8 : R] = jnp.where(sub >= 6, rows, got_fwd[f, R - 8 : R])
        cols = rolled(ring, -8 * f - 4, 1)
        got_fwd[f, :, 0:128] = jnp.where(lane < 2, cols, got_fwd[f, :, 0:128])
        got_fwd[f, :, C - 128 : C] = jnp.where(lane >= 126, cols, got_fwd[f, :, C - 128 : C])
        out_ref[0, f] = mw_v[f] * (x_ext[f, 0:R, 0:C] - got_fwd[f]) + h_ext[f, 0:R, 0:C]

    for dw in range(2):
        for d, ok, _ in copies(dw):

            @pl.when(ok)
            def _(d=d, dw=dw):
                message(d, dw).wait_send()

    @pl.when(has_next)
    def _():
        first.wait_send()
        late[0].wait_send()
        late[1].wait_send()

    @pl.when(has_prev)
    def _():
        bulk[0].wait_send()
        bulk[1].wait_send()


def per_device(sizes, *args):
    args = args[:3] + (jnp.transpose(args[3], (1, 0, 2)),) + args[4:]
    R, C = args[0].shape[-2:]
    count = args[4].shape[-1]
    ext = (R + 8, C + 128)
    vmem = lambda *shape: pltpu.VMEM(shape, F32)
    anywhere = pl.BlockSpec(memory_space=pl.ANY)
    return pl.pallas_call(
        functools.partial(kernel, sizes),
        out_shape=jax.ShapeDtypeStruct(args[0].shape, F32),
        in_specs=[anywhere] * 6,
        out_specs=pl.BlockSpec(memory_space=pltpu.VMEM),
        scratch_shapes=[
            vmem(3, *ext), vmem(2, *ext), vmem(3, *ext), vmem(4, *ext), vmem(3, *ext), vmem(3, *ext), vmem(3, *ext),
            vmem(3, R, C), pltpu.SMEM((3, 1, 3), F32), pltpu.VMEM((1, count), jnp.int32), vmem(3, 1, count),
            vmem(R, 128), vmem(R // 2, 128), vmem(R // 2, 128), vmem(2, 3, 8, C), vmem(2, 2, 8, C),
            vmem(3, R, C), vmem(3, 8, C), vmem(R // 4, 128),
            vmem(2, 3, 8, C), vmem(2, 2, 8, C), vmem(2, 2, R // 2, 128), vmem(2, 4, 8, 128),
            vmem(3, R, C), vmem(3, R, C), vmem(3, R, C), vmem(3, 8, C), vmem(R // 4, 128),
            pltpu.SemaphoreType.DMA((6,)), pltpu.SemaphoreType.DMA((2, 8)), pltpu.SemaphoreType.DMA((2, 8)),
            pltpu.SemaphoreType.DMA((5,)), pltpu.SemaphoreType.DMA((5,)),
        ],
        compiler_params=pltpu.CompilerParams(
            collective_id=0, has_side_effects=True, vmem_limit_bytes=60 * 1024 * 1024
        ),
        cost_estimate=pl.CostEstimate(flops=10_000_000, bytes_accessed=1_000_000, transcendentals=0),
        name="window_product",
    )(*args)


def solution(mesh):
    sizes = tuple(mesh.shape[name] for name in ("win", "lat", "lon"))
    in_specs = (
        P("win", None, "lat", "lon"),
        P("win", None, "lat", "lon"),
        P("win", None, "lat", "lon"),
        P("win", None, None),
        P("win", "lat", "lon", None),
        P("win", None, "lat", "lon", None),
    )
    out_specs = P("win", None, "lat", "lon")
    return jax.shard_map(
        functools.partial(per_device, sizes), mesh=mesh, in_specs=in_specs, out_specs=out_specs, check_vma=False
    )
```

time: 331 us -> 44.9 us (0.14)
  starting transfers between devices: 210 us -> 0 us
  waiting for transfers between devices: 81.1 us -> 0 us
  Pallas kernels: 0 us -> 43.1 us
  other arithmetic: 24.3 us -> 0 us
  local copies, waits for them, and re-layouts: 14.2 us -> 1.62 us
    ppermute x22 -> x0, starting transfers between devices: 210 us -> none  [the longest x10 110 us: extended_2(): lax.ppermute(lax.slice_in_dim(block, 0, width, axis=dim), axis, backward)]
    ppermute x22 -> x0, waiting for transfers between devices: 81.1 us -> none  [the longest x10 75.4 us: extended_2(): lax.ppermute(lax.slice_in_dim(block, 0, width, axis=dim), axis, backward)]
    pallas_call x0 -> x1, Pallas kernels: none -> 43.1 us  [per_device(): pl.pallas_call(functools.partial(kernel, sizes), out_shape=jax.ShapeDtype...]
    scatter-add x1 -> x0, other arithmetic: 16.1 us -> none  [per_device(): placed = jnp.zeros_like(flat).at[:, cells].add(obs_scale * picked)]
    reshape x1 -> x0, local copies, waits for them, and re-layouts: 5.23 us -> none  [per_device(): observed = placed.reshape(forward.shape)]
    add x1 -> x0, local copies, waits for them, and re-layouts: 4.67 us -> none  [tangent_core(): return clear_rims(result + mixing(mixer, center))]
  transfers between devices with their start and end apart: 22 -> 0, of which waited for: 12 -> 0; matrix products, arithmetic and copies ran while one was open for 10% -> 0% of each run, Pallas kernels for 0% -> 0%
where the time goes in v1:
time: 44.9 us; the launch traced here: 44.7 us
  Pallas kernels  43.1 us (96%)
  local copies, waits for them, and re-layouts  1.62 us (4%)
    pallas_call x1, Pallas kernels, per_device(): pl.pallas_call(functools.partial(kernel, sizes), out_shape=jax.ShapeDtype...  43.1 us
    unnamed x1, local copies, waits for them, and re-layouts  1.62 us

profile of v1, /device:TPU:31, one launch (start us, length us, event | category | flops | bytes accessed | tf_op | source)
XLA Modules:
  0.0 44.7 jit_solution(28443329825092507)
XLA Ops:
  0.0 43.1 %window_product.1 = f32[1,3,64,256]{3,2,1,0:T(8,128)} custom-call(f32[1,3,64,256]{3,2,1,0:T(8,128)} %inc_h.1, f32[1,3,64,256]{3,2,1,0:T(8,128)} %mw_h.1, f32[1,2,64,256]{3,2,1,0:T(8,128)} %winds_h.1, f32[3,1,3]{2,1,0:T(1,128)} %bitcast.1, s32[1,1,1,1024]{3,2,1,0:T(1,128)} %cells_h.1, f32[1,3,1,1,1024]{4,3,2,1,0:T(1,128)} %ow_h.1), custom_call_target="tpu_custom_call" | custom-call | flops 10000000 | bytes 1000000 | tf_op jit(solution)/shard_map/window_product/pallas_call | solution.py:400
  43.1 1.6 %copy.8 = f32[1,3,64,256]{3,2,1,0:T(8,128)} copy(f32[1,3,64,256]{3,2,1,0:T(8,128)} %window_product.1) | data formatting | bytes 393216

commit v2 on v1

--- a/solution.py
+++ b/solution.py
@@ -66,9 +66,9 @@
     out_ref,
     x_ext, u_ext, w_ext, coef, g_ext, h_ext, t_ext,
     mw_v, rea_s, cells_v, ow_v,
-    pack, ce, cw, rows_own, rows_far, fwd0, ring_r, ring_c,
+    pack, cols, rows_own, rows_far, fwd0, ring_r, ring_c,
     got_rows_own, got_rows_far, got_cols, got_corner, inc_n, mw_n, got_fwd, got_ring_r, got_ring_c,
-    load_sem, send_sem, recv_sem, xsend_sem, xrecv_sem,
+    load_sem, send_sem, recv_sem, xsend_sem, xrecv_sem, gate, far_ok,
 ):
     n_win, n_lat, n_lon = sizes
     win, lat, lon = lax.axis_index("win"), lax.axis_index("lat"), lax.axis_index("lon")
@@ -81,19 +81,49 @@
         return (lat + step >= 0) & (lat + step < n_lat)
 
     has_prev, has_next = win > 0, win < n_win - 1
-
-    barrier = pltpu.get_barrier_semaphore()
-
-    def tell(ok, target):
-        @pl.when(ok)
-        def _():
-            pl.semaphore_signal(barrier, inc=1, device_id=target, device_id_type=MESH)
-
-    for dlat, dlon in DIRS:
-        tell(lat_ok(-dlat), (win, lat - dlat, lon_at(-dlon)))
-        tell(has_next & lat_ok(-dlat), (win + 1, lat - dlat, lon_at(-dlon)))
-    tell(has_next, (win + 1, lat, lon))
-    tell(has_prev, (win - 1, lat, lon))
+    mid = n_lat // 2
+
+    def is_last(at_lat, at_lon):
+        return (at_lat == mid - 1) & (at_lon == n_lon - 1)
+
+    def is_first(at_lat, at_lon):
+        return (at_lat == mid) & (at_lon == 0)
+
+    def meets_origin(at_win, at_lat, at_lon):
+        return (at_win < 2) & (at_lat < 2) & (at_lon == n_lon - 1)
+
+    def deferred(at_win, at_lat, at_lon, d, dw):
+        dlat, dlon = DIRS[d]
+        held = lat < 0
+        if dlat == 1 and dlon <= 0:
+            held = held | is_last(at_lat, at_lon)
+        if dlon == -1 and dlat >= 0:
+            held = held | is_first(at_lat, at_lon)
+        if dlon == 1 and dlat <= 0:
+            held = held | ((at_win == dw) & (at_lat == -dlat) & (at_lon == n_lon - 1))
+        return held
+
+    def answered(at_win, at_lat, at_lon, d):
+        dlat, dlon = DIRS[d]
+        early = lat < 0
+        if dlon == -1:
+            early = early | ((at_lon == 0) & (at_lat < mid) & (at_lat + dlat < mid))
+        if dlat == 1:
+            early = early | ((at_lat == mid - 1) & (at_lon < n_lon // 2))
+        return early & ((at_win > 0) | (at_lat > 0) | (at_lon > 0))
+
+    def turn(d):
+        dlat, dlon = DIRS[d]
+        urgent = later = lat < 0
+        if dlat == -1:
+            urgent = urgent | (lat == mid)
+        if dlon == 1:
+            urgent = urgent | (lon == n_lon - 1)
+        if dlat == 1:
+            later = later | (lat == mid - 1)
+        if dlon == -1:
+            later = later | (lon == 0)
+        return jnp.where(urgent, 0, jnp.where(later, 2, 1))
 
     tile = (slice(None), pl.ds(0, R), pl.ds(0, C))
     loads = [
@@ -107,6 +137,25 @@
     for load in loads:
         load.start()
 
+    barrier = pltpu.get_barrier_semaphore()
+
+    def tell(ok, target):
+        @pl.when(ok)
+        def _():
+            pl.semaphore_signal(barrier, inc=1, device_id=target, device_id_type=MESH)
+
+    for d, (dlat, dlon) in enumerate(DIRS):
+        for dw in range(2):
+            source = (win + dw, lat - dlat, lon_at(-dlon))
+            ok = lat_ok(-dlat) & jnp.logical_not(deferred(*source, d, dw) | answered(*source, d))
+            tell(ok & has_next if dw else ok, source)
+        tell(has_prev & lat_ok(dlat) & answered(win, lat, lon, d), (win - 1, lat + dlat, lon_at(dlon)))
+    origin = (win == 0) & (lat == 0) & (lon == 0)
+    tell(origin, (win, lat, lon_at(-2)))
+    tell(origin & has_next, (win + 1, lat, lon_at(-2)))
+    tell(has_next, (win + 1, lat, lon))
+    tell(has_prev, (win - 1, lat, lon))
+
     for d, (dlat, dlon) in enumerate(DIRS):
         for dw in range(2):
             there = lat_ok(-dlat) & (has_next if dw else (win >= 0))
@@ -157,15 +206,21 @@
 
     lane = iota((R, 128), 1)
     packed = jnp.zeros((R, 128), F32)
-    own = [(x_ext, 0), (x_ext, 1), (x_ext, 2), (u_ext, 0), (u_ext, 1), (w_ext, 0), (w_ext, 1), (w_ext, 2), (mw_v, 0), (mw_v, 1), (mw_v, 2)]
+    own = [(x_ext, 0), (x_ext, 1), (x_ext, 2), (u_ext, 0), (u_ext, 1), (w_ext, 0), (w_ext, 1), (w_ext, 2), (mw_v, 0), (mw_v, 1), (mw_v, 2), (x_ext, 0), (x_ext, 1), (x_ext, 2)]
     for a, (ref, f) in enumerate(own):
         ends = jnp.where(lane < 64, ref[f, 0:R, 0:128], ref[f, 0:R, C - 128 : C])
         packed = jnp.where((lane >= 8 * a) & (lane < 8 * a + 8), rolled(ends, 8 * a + 4, 1), packed)
     pack[...] = packed
     half = R // 2
     low_lane = lax.rem(iota((half, 128), 1), 8) < 4
-    ce[...] = jnp.where(low_lane, packed[:half], rolled(packed[half:], 4, 1))
-    cw[...] = jnp.where(low_lane, rolled(packed[half:], -4, 1), packed[:half])
+    left = iota((half // 2, 128), 1) < 64
+    for e, pair in enumerate((
+        jnp.where(low_lane, packed[:half], rolled(packed[half:], 4, 1)),
+        jnp.where(low_lane, rolled(packed[half:], -4, 1), packed[:half]),
+    )):
+        upper, lower = pair[: half // 2], pair[half // 2 :]
+        cols[0, e] = jnp.where(left, upper, rolled(lower, 64, 1))
+        cols[1, e] = jnp.where(left, rolled(upper, 64, 1), lower)
 
     sub = iota((8, C), 0)
     lu, lv = u_ext[0, R - 8 : R, 0:C], u_ext[1, R - 8 : R, 0:C]
@@ -190,28 +245,24 @@
         rows_far[0, pair] = n_rows
         rows_far[1, pair] = n_cols
 
-    uc, vc = u_ext[0, 0:R, 0:C], u_ext[1, 0:R, 0:C]
-    coef[0, 0:R, 0:C] = DIFFUSION - uc
-    coef[1, 0:R, 0:C] = DIFFUSION + uc
-    coef[2, 0:R, 0:C] = DIFFUSION - vc
-    coef[3, 0:R, 0:C] = DIFFUSION + vc
-    c_tile = [coef[i, 0:R, 0:C] for i in range(4)]
-    state = [x_ext[f, 0:R, 0:C] for f in range(3)]
-    for _ in range(2):
-        state = tangent(state, c_tile, mix)
-    for f in range(3):
-        fwd0[f] = state[f]
-
     lats = 1 + lat_ok(1).astype(jnp.int32) + lat_ok(-1).astype(jnp.int32)
     prev, nxt = has_prev.astype(jnp.int32), has_next.astype(jnp.int32)
-    pl.semaphore_wait(barrier, 3 * lats * (1 + prev) - 1 + nxt)
+    ends = (is_last(lat, lon) | is_first(lat, lon)).astype(jnp.int32)
+    meets = meets_origin(win, lat, lon).astype(jnp.int32)
+    knows_origin = (win < 2) & (lat == 0) & (lon == n_lon - 2)
+    asks = owed = jnp.int32(0)
+    for d, (dlat, dlon) in enumerate(DIRS):
+        asks += (lat_ok(dlat) & answered(win, lat, lon, d)).astype(jnp.int32)
+        owed += (lat_ok(-dlat) & answered(win + 1, lat - dlat, lon_at(-dlon), d)).astype(jnp.int32)
+    others = (3 * lats - 2 * ends - asks) * (1 + prev) - 1 + nxt + owed * nxt
+    pl.semaphore_wait(barrier, others - meets + knows_origin.astype(jnp.int32))
 
     def message(d, dw):
         dlat, dlon = DIRS[d]
         if dlon == 0:
             src, dst = (rows_far.at[d], got_rows_far.at[d]) if dw else (rows_own.at[d], got_rows_own.at[d])
         elif dlat == 0:
-            src, dst = (ce if dlon == 1 else cw), got_cols.at[dw, d - 2]
+            src, dst = cols.at[dw, d - 2], got_cols.at[dw, d - 2]
         else:
             src, dst = pack.at[pl.ds(R - 8 if dlat == 1 else 0, 8)], got_corner.at[dw, d - 4]
         return pltpu.make_async_remote_copy(
@@ -237,48 +288,111 @@
         for d, (dlat, _) in enumerate(DIRS):
             yield d, lat_ok(dlat) & (has_prev if dw else (win >= 0)), lat_ok(-dlat) & (has_next if dw else (win >= 0))
 
-    for dw in range(2):
-        for d, ok, _ in copies(dw):
-
-            @pl.when(ok)
-            def _(d=d, dw=dw):
-                message(d, dw).start()
+    def answer():
+        for dw in range(2):
+            for d, _, ok in copies(dw):
+                dlat, dlon = DIRS[d]
+                source = (win + dw, lat - dlat, lon_at(-dlon))
+
+                @pl.when(ok & answered(*source, d))
+                def _(source=source):
+                    pl.semaphore_signal(far_ok, inc=1, device_id=source, device_id_type=MESH)
+
+    for now in range(3):
+        for dw in range(2):
+            for d, ok, _ in copies(dw):
+
+                @pl.when(ok & (turn(d) == now) & jnp.logical_not(deferred(win, lat, lon, d, dw) | answered(win, lat, lon, d)))
+                def _(d=d, dw=dw):
+                    message(d, dw).start()
+
+        if now == 0:
+            answer()
 
     bulk = [across(0, inc_h.at[0], inc_n, -1), across(1, mw_h.at[0], mw_n, -1)]
     first = across(2, fwd0, got_fwd, 1)
     late = [across(3, ring_r, got_ring_r, 1), across(4, ring_c, got_ring_c, 1)]
 
-    @pl.when(has_next)
-    def _():
-        first.start()
-
     @pl.when(has_prev)
     def _():
         bulk[0].start()
         bulk[1].start()
 
-    for dw in range(2):
+    @pl.when((lat == mid - 1) & (lon == n_lon - 2))
+    def _():
+        pl.semaphore_signal(gate, inc=1, device_id=(win, lat, lon + 1), device_id_type=MESH)
+
+    @pl.when(knows_origin)
+    def _():
+        pl.semaphore_signal(gate, inc=1, device_id=(win, lat, lon + 1), device_id_type=MESH)
+        pl.semaphore_signal(gate, inc=1, device_id=(win, lat + 1, lon + 1), device_id_type=MESH)
+
+    @pl.when((lat == mid + 1) & (lon == 0))
+    def _():
+        pl.semaphore_signal(gate, inc=1, device_id=(win, lat - 1, lon), device_id_type=MESH)
+
+    uc, vc = u_ext[0, 0:R, 0:C], u_ext[1, 0:R, 0:C]
+    coef[0, 0:R, 0:C] = DIFFUSION - uc
+    coef[1, 0:R, 0:C] = DIFFUSION + uc
+    coef[2, 0:R, 0:C] = DIFFUSION - vc
+    coef[3, 0:R, 0:C] = DIFFUSION + vc
+    c_tile = [coef[i, 0:R, 0:C] for i in range(4)]
+    state = [x_ext[f, 0:R, 0:C] for f in range(3)]
+    for _ in range(2):
+        state = tangent(state, c_tile, mix)
+    for f in range(3):
+        fwd0[f] = state[f]
+
+    @pl.when(has_next)
+    def _():
+        first.start()
+
+    @pl.when(ends + meets > 0)
+    def _():
+        pl.semaphore_wait(gate, ends + meets)
+        for dw in range(2):
+            for d, ok, _ in copies(dw):
+
+                @pl.when(ok & deferred(win, lat, lon, d, dw))
+                def _(d=d, dw=dw):
+                    message(d, dw).start()
+
+    @pl.when(asks > 0)
+    def _():
+        pl.semaphore_wait(far_ok, asks * (1 + prev))
+        for dw in range(2):
+            for d, ok, _ in copies(dw):
+
+                @pl.when(ok & answered(win, lat, lon, d))
+                def _(d=d, dw=dw):
+                    message(d, dw).start()
+
+    def arrive(dw):
         for d, _, ok in copies(dw):
 
             @pl.when(ok)
             def _(d=d, dw=dw):
                 message(d, dw).wait_recv()
 
+    arrive(0)
+
     corner_low = lax.rem(iota((8, 128), 1), 8) < 4
     corner_sub = iota((8, 128), 0)
 
     def columns(dw):
-        from_west, from_east = got_cols[dw, 0], got_cols[dw, 1]
+        from_west, from_east = (
+            jnp.concatenate([got_cols[dw, i], rolled(got_cols[dw, i], 64, 1)], axis=0) for i in range(2)
+        )
         upper = jnp.where(low_lane, from_west, from_east)
         lower = jnp.where(low_lane, rolled(from_west, -4, 1), rolled(from_east, 4, 1))
         sw, se, nw, ne = (got_corner[dw, i] for i in range(4))
         rim = jnp.where(corner_sub < 4, jnp.where(corner_low, nw, ne), jnp.where(corner_low, sw, se))
-        return jnp.concatenate([upper, lower, rim], axis=0)
+        return jnp.concatenate([upper, lower, rolled(rim, 64, 1) if dw else rim], axis=0)
 
     own_cols = columns(0)
 
-    def side(cols, a):
-        return rolled(cols, -8 * a - 4, 1)
+    def side(ends, a):
+        return rolled(ends, -8 * a - 4, 1)
 
     E = R + 8
     inside = jnp.where(iota((8, C), 0) < 4, lat_ok(1).astype(F32), lat_ok(-1).astype(F32)) > 0.0
@@ -295,8 +409,8 @@
             rows = jnp.where(sub == 5 + t, rolled(got_rows_own[0, t], 5 + t - i, 0), rows)
         coef[2 * i, R:E, 0:C] = jnp.where(inside, DIFFUSION - rows, 0.0)
         coef[2 * i + 1, R:E, 0:C] = jnp.where(inside, DIFFUSION + rows, 0.0)
-        cols = side(own_cols, 3 + i)
-        less, more = DIFFUSION - cols, DIFFUSION + cols
+        ends = side(own_cols, 3 + i)
+        less, more = DIFFUSION - ends, DIFFUSION + ends
         coef[2 * i, 0:R, C:] = less[0:R]
         coef[2 * i + 1, 0:R, C:] = more[0:R]
         coef[2 * i, R:E, C:] = jnp.where(inside[:, 0:128], less[R:E], 0.0)
@@ -326,6 +440,7 @@
         late[0].start()
         late[1].start()
 
+    arrive(1)
     far_cols = columns(1)
 
     @pl.when(has_next)
@@ -338,13 +453,13 @@
         south_rows, north_rows = got_rows_far[0, t], got_rows_far[1, t]
         inc_rows = jnp.where(sub < 4, rolled(north_rows, -base, 0), rolled(south_rows, base, 0))
         mw_rows = jnp.where(sub < 4, rolled(north_rows, -base - 2, 0), rolled(south_rows, base + 2, 0))
-        mw_cols = side(far_cols, 8 + f)
+        mw_cols = side(far_cols, f)
         g_ext[f, 0:R, 0:C] = w_ext[f, 0:R, 0:C] + mw_n[f]
         h_ext[f, 0:R, 0:C] = mw_n[f] * inc_n[f]
         g_ext[f, R:E, 0:C] = w_ext[f, R:E, 0:C] + mw_rows
         h_ext[f, R:E, 0:C] = mw_rows * inc_rows
         g_ext[f, :, C:] = w_ext[f, :, C:] + mw_cols
-        h_ext[f, :, C:] = mw_cols * side(far_cols, f)
+        h_ext[f, :, C:] = mw_cols * side(far_cols, 3 + f)
 
     state = [g_ext[f] * t_ext[f] - h_ext[f] for f in range(3)]
     state = adjoint(state, c_all, mix)
@@ -366,9 +481,9 @@
         rows = got_ring_r[f]
         got_fwd[f, 0:8] = jnp.where(sub < 2, rows, got_fwd[f, 0:8])
         got_fwd[f, R - 8 : R] = jnp.where(sub >= 6, rows, got_fwd[f, R - 8 : R])
-        cols = rolled(ring, -8 * f - 4, 1)
-        got_fwd[f, :, 0:128] = jnp.where(lane < 2, cols, got_fwd[f, :, 0:128])
-        got_fwd[f, :, C - 128 : C] = jnp.where(lane >= 126, cols, got_fwd[f, :, C - 128 : C])
+        ends = rolled(ring, -8 * f - 4, 1)
+        got_fwd[f, :, 0:128] = jnp.where(lane < 2, ends, got_fwd[f, :, 0:128])
+        got_fwd[f, :, C - 128 : C] = jnp.where(lane >= 126, ends, got_fwd[f, :, C - 128 : C])
         out_ref[0, f] = mw_v[f] * (x_ext[f, 0:R, 0:C] - got_fwd[f]) + h_ext[f, 0:R, 0:C]
 
     for dw in range(2):
@@ -394,6 +509,7 @@
     args = args[:3] + (jnp.transpose(args[3], (1, 0, 2)),) + args[4:]
     R, C = args[0].shape[-2:]
     count = args[4].shape[-1]
+    args = [pltpu.with_memory_space_constraint(a, pltpu.HBM) for a in args]
     ext = (R + 8, C + 128)
     vmem = lambda *shape: pltpu.VMEM(shape, F32)
     anywhere = pl.BlockSpec(memory_space=pl.ANY)
@@ -405,15 +521,16 @@
         scratch_shapes=[
             vmem(3, *ext), vmem(2, *ext), vmem(3, *ext), vmem(4, *ext), vmem(3, *ext), vmem(3, *ext), vmem(3, *ext),
             vmem(3, R, C), pltpu.SMEM((3, 1, 3), F32), pltpu.VMEM((1, count), jnp.int32), vmem(3, 1, count),
-            vmem(R, 128), vmem(R // 2, 128), vmem(R // 2, 128), vmem(2, 3, 8, C), vmem(2, 2, 8, C),
+            vmem(R, 128), vmem(2, 2, R // 4, 128), vmem(2, 3, 8, C), vmem(2, 2, 8, C),
             vmem(3, R, C), vmem(3, 8, C), vmem(R // 4, 128),
-            vmem(2, 3, 8, C), vmem(2, 2, 8, C), vmem(2, 2, R // 2, 128), vmem(2, 4, 8, 128),
+            vmem(2, 3, 8, C), vmem(2, 2, 8, C), vmem(2, 2, R // 4, 128), vmem(2, 4, 8, 128),
             vmem(3, R, C), vmem(3, R, C), vmem(3, R, C), vmem(3, 8, C), vmem(R // 4, 128),
             pltpu.SemaphoreType.DMA((6,)), pltpu.SemaphoreType.DMA((2, 8)), pltpu.SemaphoreType.DMA((2, 8)),
-            pltpu.SemaphoreType.DMA((5,)), pltpu.SemaphoreType.DMA((5,)),
+            pltpu.SemaphoreType.DMA((5,)), pltpu.SemaphoreType.DMA((5,)), pltpu.SemaphoreType.REGULAR,
+            pltpu.SemaphoreType.REGULAR,
         ],
         compiler_params=pltpu.CompilerParams(
-            collective_id=0, has_side_effects=True, vmem_limit_bytes=60 * 1024 * 1024
+            collective_id=0, has_side_effects=True, vmem_limit_bytes=32 * 1024 * 1024
         ),
         cost_estimate=pl.CostEstimate(flops=10_000_000, bytes_accessed=1_000_000, transcendentals=0),
         name="window_product",

time: 44.9 us -> 38.9 us (0.87)
  the two profiles are of different devices: /device:TPU:31 before, /device:TPU:2 now
where the time goes in v2:
time: 38.9 us; the launch traced here: 38.7 us
  Pallas kernels  38 us (98%)
  local copies, waits for them, and re-layouts  0.68 us (2%)
    pallas_call x1, Pallas kernels, per_device(): pl.pallas_call(functools.partial(kernel, sizes), out_shape=jax.ShapeDtype...  38 us

profile of v2, /device:TPU:2, one launch (start us, length us, event | category | flops | bytes accessed | tf_op | source)
XLA Modules:
  0.0 38.7 jit_solution(8199727504697630558)
XLA Ops:
  0.0 38.0 %window_product.1 = f32[1,3,64,256]{3,2,1,0:T(8,128)S(1)} custom-call(f32[1,3,64,256]{3,2,1,0:T(8,128)} %inc_h.1, f32[1,3,64,256]{3,2,1,0:T(8,128)} %mw_h.1, f32[1,2,64,256]{3,2,1,0:T(8,128)} %winds_h.1, f32[3,1,3]{2,1,0:T(1,128)} %bitcast.1, s32[1,1,1,1024]{3,2,1,0:T(1,128)} %cells_h.1, f32[1,3,1,1,1024]{4,3,2,1,0:T(1,128)} %ow_h.1), custom_call_target="tpu_custom_call" | custom-call | flops 10000000 | bytes 1000000 | tf_op jit(solution)/shard_map/window_product/pallas_call | solution.py:516
  38.0 0.7 %copy.8 = f32[1,3,64,256]{3,2,1,0:T(8,128)} copy(f32[1,3,64,256]{3,2,1,0:T(8,128)S(1)} %window_product.1) | data formatting | bytes 393216

commit v3 on v2

--- a/solution.py
+++ b/solution.py
@@ -68,7 +68,8 @@
     mw_v, rea_s, cells_v, ow_v,
     pack, cols, rows_own, rows_far, fwd0, ring_r, ring_c,
     got_rows_own, got_rows_far, got_cols, got_corner, inc_n, mw_n, got_fwd, got_ring_r, got_ring_c,
-    load_sem, send_sem, recv_sem, xsend_sem, xrecv_sem, gate, far_ok,
+    load_sem, send_sem, recv_sem, xsend_sem, xrecv_sem, fsend_sem, frecv_sem, gate, far_ok,
+    prev_rows, prev_cols, prev_corner, prev_inc, prev_wind, prev_rea, prev_rea_s, xp_ext, cp_ext,
 ):
     n_win, n_lat, n_lon = sizes
     win, lat, lon = lax.axis_index("win"), lax.axis_index("lat"), lax.axis_index("lon")
@@ -88,6 +89,9 @@
 
     def is_first(at_lat, at_lon):
         return (at_lat == mid) & (at_lon == 0)
+
+    def is_corner(at_lat, at_lon):
+        return (at_lat == mid) & (at_lon == n_lon - 1)
 
     def meets_origin(at_win, at_lat, at_lon):
         return (at_win < 2) & (at_lat < 2) & (at_lon == n_lon - 1)
@@ -99,6 +103,8 @@
             held = held | is_last(at_lat, at_lon)
         if dlon == -1 and dlat >= 0:
             held = held | is_first(at_lat, at_lon)
+        if (dlat == -1 and dlon <= 0) or (dlon == 1 and dlat >= 0):
+            held = held | is_corner(at_lat, at_lon)
         if dlon == 1 and dlat <= 0:
             held = held | ((at_win == dw) & (at_lat == -dlat) & (at_lon == n_lon - 1))
         return held
@@ -151,6 +157,14 @@
             tell(ok & has_next if dw else ok, source)
         tell(has_prev & lat_ok(dlat) & answered(win, lat, lon, d), (win - 1, lat + dlat, lon_at(dlon)))
     origin = (win == 0) & (lat == 0) & (lon == 0)
+    follower = (win == 1) & (lat == 0) & (lon == 0)
+    feeds = {
+        d: has_next & (win == 0) & (lat == -dlat) & (lon_at(dlon) == 0)
+        for d, (dlat, dlon) in enumerate(DIRS)
+        if dlat <= 0
+    }
+    for d in feeds:
+        tell(follower, (win - 1, lat - DIRS[d][0], lon_at(-DIRS[d][1])))
     tell(origin, (win, lat, lon_at(-2)))
     tell(origin & has_next, (win + 1, lat, lon_at(-2)))
     tell(has_next, (win + 1, lat, lon))
@@ -170,6 +184,13 @@
                     ref = got_corner.at[dw, d - 4]
                 ref[...] = jnp.zeros(ref.shape, F32)
 
+    @pl.when(follower)
+    def _():
+        prev_rows[0] = jnp.zeros(prev_rows.shape[1:], F32)
+        for i, (dlat, _) in enumerate(DIRS[4:]):
+            if dlat > 0:
+                prev_corner[i] = jnp.zeros(prev_corner.shape[1:], F32)
+
     @pl.when(jnp.logical_not(has_next))
     def _():
         inc_n[...] = jnp.zeros(inc_n.shape, F32)
@@ -178,8 +199,6 @@
     @pl.when(jnp.logical_not(has_prev))
     def _():
         got_fwd[...] = jnp.zeros(got_fwd.shape, F32)
-        got_ring_r[...] = jnp.zeros(got_ring_r.shape, F32)
-        got_ring_c[...] = jnp.zeros(got_ring_c.shape, F32)
 
     loads[0].wait()
     loads[1].wait()
@@ -189,16 +208,19 @@
     col_of = lax.bitwise_and(cells, 255)
     at_row = iota((R, count), 0) == row_of
     at_col = jnp.where(iota((C, count), 0) == col_of, 1.0, 0.0).astype(BF16)
+    spread = []
     for f in range(3):
         rest = ow_v[f]
-        total = None
         for _ in range(3):
             part = rest.astype(BF16).astype(F32)
             rest = rest - part
-            spread = jnp.where(at_row, part, 0.0).astype(BF16)
-            term = lax.dot_general(spread, at_col, (((1,), (1,)), ((), ())), preferred_element_type=F32)
-            total = term if total is None else total + term
-        w_ext[f, 0:R, 0:C] = total
+            spread.append(jnp.where(at_row, part, 0.0).astype(BF16))
+    sums = lax.dot_general(
+        jnp.concatenate(spread, axis=0), at_col, (((1,), (1,)), ((), ())), preferred_element_type=F32
+    )
+    for f in range(3):
+        top, low, rest = (sums[R * (3 * f + p) : R * (3 * f + p + 1)] for p in range(3))
+        w_ext[f, 0:R, 0:C] = top + low + rest
 
     for load in loads[2:]:
         load.wait()
@@ -254,8 +276,27 @@
     for d, (dlat, dlon) in enumerate(DIRS):
         asks += (lat_ok(dlat) & answered(win, lat, lon, d)).astype(jnp.int32)
         owed += (lat_ok(-dlat) & answered(win + 1, lat - dlat, lon_at(-dlon), d)).astype(jnp.int32)
-    others = (3 * lats - 2 * ends - asks) * (1 + prev) - 1 + nxt + owed * nxt
-    pl.semaphore_wait(barrier, others - meets + knows_origin.astype(jnp.int32))
+    fed = functools.reduce(jnp.add, [feed.astype(jnp.int32) for feed in feeds.values()])
+    corner = is_corner(lat, lon).astype(jnp.int32)
+    others = (3 * lats - 2 * ends - 4 * corner - asks) * (1 + prev) - 1 + nxt + owed * nxt
+    pl.semaphore_wait(barrier, others - meets + knows_origin.astype(jnp.int32) + fed)
+
+    def feed_message(d):
+        dlat, dlon = DIRS[d]
+        if dlon == 0:
+            src, dst = rows_own.at[d], prev_rows.at[d]
+        elif dlat == 0:
+            src, dst = cols.at[0, d - 2], prev_cols.at[d - 2]
+        else:
+            src, dst = pack.at[pl.ds(R - 8 if dlat == 1 else 0, 8)], prev_corner.at[d - 4]
+        return pltpu.make_async_remote_copy(
+            src_ref=src,
+            dst_ref=dst,
+            send_sem=fsend_sem.at[d],
+            recv_sem=frecv_sem.at[d],
+            device_id=(win + 1, lat + dlat, lon_at(dlon)),
+            device_id_type=MESH,
+        )
 
     def message(d, dw):
         dlat, dlon = DIRS[d]
@@ -294,6 +335,7 @@
                 dlat, dlon = DIRS[d]
                 source = (win + dw, lat - dlat, lon_at(-dlon))
 
+
                 @pl.when(ok & answered(*source, d))
                 def _(source=source):
                     pl.semaphore_signal(far_ok, inc=1, device_id=source, device_id_type=MESH)
@@ -312,13 +354,22 @@
     bulk = [across(0, inc_h.at[0], inc_n, -1), across(1, mw_h.at[0], mw_n, -1)]
     first = across(2, fwd0, got_fwd, 1)
     late = [across(3, ring_r, got_ring_r, 1), across(4, ring_c, got_ring_c, 1)]
-
-    @pl.when(has_prev)
-    def _():
-        bulk[0].start()
-        bulk[1].start()
-
-    @pl.when((lat == mid - 1) & (lon == n_lon - 2))
+    origin_own = [across(5, inc_h.at[0], prev_inc, 1), across(6, winds_h.at[0], prev_wind, 1), across(7, rea_h, prev_rea, 1)]
+    to_next = has_next & jnp.logical_not(origin)
+    from_prev = has_prev & jnp.logical_not(follower)
+
+    for d, feed in feeds.items():
+
+        @pl.when(feed)
+        def _(d=d):
+            feed_message(d).start()
+
+    @pl.when(origin & has_next)
+    def _():
+        for copy in origin_own:
+            copy.start()
+
+    @pl.when(((lat == mid - 1) | (lat == mid)) & (lon == n_lon - 2))
     def _():
         pl.semaphore_signal(gate, inc=1, device_id=(win, lat, lon + 1), device_id_type=MESH)
 
@@ -327,7 +378,7 @@
         pl.semaphore_signal(gate, inc=1, device_id=(win, lat, lon + 1), device_id_type=MESH)
         pl.semaphore_signal(gate, inc=1, device_id=(win, lat + 1, lon + 1), device_id_type=MESH)
 
-    @pl.when((lat == mid + 1) & (lon == 0))
+    @pl.when((lat == mid + 1) & ((lon == 0) | (lon == n_lon - 1)))
     def _():
         pl.semaphore_signal(gate, inc=1, device_id=(win, lat - 1, lon), device_id_type=MESH)
 
@@ -343,13 +394,18 @@
     for f in range(3):
         fwd0[f] = state[f]
 
-    @pl.when(has_next)
+    @pl.when(to_next)
     def _():
         first.start()
 
-    @pl.when(ends + meets > 0)
-    def _():
-        pl.semaphore_wait(gate, ends + meets)
+    @pl.when(has_prev)
+    def _():
+        bulk[0].start()
+        bulk[1].start()
+
+    @pl.when(ends + meets + corner > 0)
+    def _():
+        pl.semaphore_wait(gate, ends + meets + 2 * corner)
         for dw in range(2):
             for d, ok, _ in copies(dw):
 
@@ -379,42 +435,45 @@
     corner_low = lax.rem(iota((8, 128), 1), 8) < 4
     corner_sub = iota((8, 128), 0)
 
-    def columns(dw):
+    def columns(from_cols, from_corner, far):
         from_west, from_east = (
-            jnp.concatenate([got_cols[dw, i], rolled(got_cols[dw, i], 64, 1)], axis=0) for i in range(2)
+            jnp.concatenate([from_cols[i], rolled(from_cols[i], 64, 1)], axis=0) for i in range(2)
         )
         upper = jnp.where(low_lane, from_west, from_east)
         lower = jnp.where(low_lane, rolled(from_west, -4, 1), rolled(from_east, 4, 1))
-        sw, se, nw, ne = (got_corner[dw, i] for i in range(4))
+        sw, se, nw, ne = (from_corner[i] for i in range(4))
         rim = jnp.where(corner_sub < 4, jnp.where(corner_low, nw, ne), jnp.where(corner_low, sw, se))
-        return jnp.concatenate([upper, lower, rolled(rim, 64, 1) if dw else rim], axis=0)
-
-    own_cols = columns(0)
+        return jnp.concatenate([upper, lower, rolled(rim, 64, 1) if far else rim], axis=0)
+
+    own_cols = columns(got_cols.at[0], got_corner.at[0], False)
 
     def side(ends, a):
         return rolled(ends, -8 * a - 4, 1)
 
     E = R + 8
     inside = jnp.where(iota((8, C), 0) < 4, lat_ok(1).astype(F32), lat_ok(-1).astype(F32)) > 0.0
-    for f in range(3):
-        south_rows, north_rows = got_rows_own[0, f], got_rows_own[1, f]
-        x_ext[f, :, C:] = side(own_cols, f)
-        x_ext[f, R:E, 0:C] = jnp.where(sub < 4, north_rows, south_rows)
+    def unpack(from_rows, ends_all, x, c):
+        for f in range(3):
+            x[f, :, C:] = side(ends_all, f)
+            x[f, R:E, 0:C] = jnp.where(sub < 4, from_rows[1, f], from_rows[0, f])
+        for i in range(2):
+            rows = jnp.zeros((8, C), F32)
+            for t in range(3):
+                rows = jnp.where(sub == t, rolled(from_rows[1, t], t - 6 - i, 0), rows)
+                rows = jnp.where(sub == 5 + t, rolled(from_rows[0, t], 5 + t - i, 0), rows)
+            c[2 * i, R:E, 0:C] = jnp.where(inside, DIFFUSION - rows, 0.0)
+            c[2 * i + 1, R:E, 0:C] = jnp.where(inside, DIFFUSION + rows, 0.0)
+            ends = side(ends_all, 3 + i)
+            less, more = DIFFUSION - ends, DIFFUSION + ends
+            c[2 * i, 0:R, C:] = less[0:R]
+            c[2 * i + 1, 0:R, C:] = more[0:R]
+            c[2 * i, R:E, C:] = jnp.where(inside[:, 0:128], less[R:E], 0.0)
+            c[2 * i + 1, R:E, C:] = jnp.where(inside[:, 0:128], more[R:E], 0.0)
+
+    unpack(got_rows_own, own_cols, x_ext, coef)
+    for f in range(3):
         w_ext[f, :, C:] = side(own_cols, 5 + f)
-        w_ext[f, R:E, 0:C] = rolled(jnp.where(sub < 4, south_rows, north_rows), 4, 0)
-    for i in range(2):
-        rows = jnp.zeros((8, C), F32)
-        for t in range(3):
-            rows = jnp.where(sub == t, rolled(got_rows_own[1, t], t - 6 - i, 0), rows)
-            rows = jnp.where(sub == 5 + t, rolled(got_rows_own[0, t], 5 + t - i, 0), rows)
-        coef[2 * i, R:E, 0:C] = jnp.where(inside, DIFFUSION - rows, 0.0)
-        coef[2 * i + 1, R:E, 0:C] = jnp.where(inside, DIFFUSION + rows, 0.0)
-        ends = side(own_cols, 3 + i)
-        less, more = DIFFUSION - ends, DIFFUSION + ends
-        coef[2 * i, 0:R, C:] = less[0:R]
-        coef[2 * i + 1, 0:R, C:] = more[0:R]
-        coef[2 * i, R:E, C:] = jnp.where(inside[:, 0:128], less[R:E], 0.0)
-        coef[2 * i + 1, R:E, C:] = jnp.where(inside[:, 0:128], more[R:E], 0.0)
+        w_ext[f, R:E, 0:C] = rolled(jnp.where(sub < 4, got_rows_own[0, f], got_rows_own[1, f]), 4, 0)
 
     c_all = [coef[i] for i in range(4)]
     state = tangent([x_ext[f] for f in range(3)], c_all, mix)
@@ -435,13 +494,13 @@
         folded = jnp.where(group >= 32 * q, rolled(ring[quarter * q : quarter * (q + 1)], 32 * q, 1), folded)
     ring_c[...] = folded
 
-    @pl.when(has_next)
+    @pl.when(to_next)
     def _():
         late[0].start()
         late[1].start()
 
     arrive(1)
-    far_cols = columns(1)
+    far_cols = columns(got_cols.at[1], got_corner.at[1], True)
 
     @pl.when(has_next)
     def _():
@@ -469,21 +528,46 @@
     for f in range(3):
         h_ext[f] = state[f]
 
-    @pl.when(has_prev)
+    @pl.when(follower)
+    def _():
+        for copy in origin_own:
+            copy.wait_recv()
+        reaction = pltpu.make_async_copy(prev_rea, prev_rea_s, load_sem.at[6])
+        reaction.start()
+        for d in feeds:
+            feed_message(d).wait_recv()
+        for f in range(3):
+            xp_ext[f, 0:R, 0:C] = prev_inc[f]
+        for i in range(2):
+            cp_ext[2 * i, 0:R, 0:C] = DIFFUSION - prev_wind[i]
+            cp_ext[2 * i + 1, 0:R, 0:C] = DIFFUSION + prev_wind[i]
+        unpack(prev_rows, columns(prev_cols, prev_corner, False), xp_ext, cp_ext)
+        reaction.wait()
+        prev_mix = [[prev_rea_s[f, 0, g] + (KEEP if f == g else 0.0) for g in range(3)] for f in range(3)]
+        c_prev = [cp_ext[i] for i in range(4)]
+        state = tangent([xp_ext[f] for f in range(3)], c_prev, prev_mix)
+        for f in range(3):
+            xp_ext[f] = state[f]
+        state = tangent([xp_ext[f] for f in range(3)], c_prev, prev_mix)
+        for f in range(3):
+            got_fwd[f] = state[f][0:R, 0:C]
+
+    @pl.when(from_prev)
     def _():
         first.wait_recv()
         late[0].wait_recv()
         late[1].wait_recv()
-
-    folded = got_ring_c[...]
-    ring = jnp.concatenate([rolled(folded, -32 * q, 1) for q in range(4)], axis=0)
-    for f in range(3):
-        rows = got_ring_r[f]
-        got_fwd[f, 0:8] = jnp.where(sub < 2, rows, got_fwd[f, 0:8])
-        got_fwd[f, R - 8 : R] = jnp.where(sub >= 6, rows, got_fwd[f, R - 8 : R])
-        ends = rolled(ring, -8 * f - 4, 1)
-        got_fwd[f, :, 0:128] = jnp.where(lane < 2, ends, got_fwd[f, :, 0:128])
-        got_fwd[f, :, C - 128 : C] = jnp.where(lane >= 126, ends, got_fwd[f, :, C - 128 : C])
+        folded = got_ring_c[...]
+        ring = jnp.concatenate([rolled(folded, -32 * q, 1) for q in range(4)], axis=0)
+        for f in range(3):
+            rows = got_ring_r[f]
+            got_fwd[f, 0:8] = jnp.where(sub < 2, rows, got_fwd[f, 0:8])
+            got_fwd[f, R - 8 : R] = jnp.where(sub >= 6, rows, got_fwd[f, R - 8 : R])
+            ends = rolled(ring, -8 * f - 4, 1)
+            got_fwd[f, :, 0:128] = jnp.where(lane < 2, ends, got_fwd[f, :, 0:128])
+            got_fwd[f, :, C - 128 : C] = jnp.where(lane >= 126, ends, got_fwd[f, :, C - 128 : C])
+
+    for f in range(3):
         out_ref[0, f] = mw_v[f] * (x_ext[f, 0:R, 0:C] - got_fwd[f]) + h_ext[f, 0:R, 0:C]
 
     for dw in range(2):
@@ -493,11 +577,22 @@
             def _(d=d, dw=dw):
                 message(d, dw).wait_send()
 
-    @pl.when(has_next)
+    @pl.when(to_next)
     def _():
         first.wait_send()
         late[0].wait_send()
         late[1].wait_send()
+
+    for d, feed in feeds.items():
+
+        @pl.when(feed)
+        def _(d=d):
+            feed_message(d).wait_send()
+
+    @pl.when(origin & has_next)
+    def _():
+        for copy in origin_own:
+            copy.wait_send()
 
     @pl.when(has_prev)
     def _():
@@ -525,9 +620,11 @@
             vmem(3, R, C), vmem(3, 8, C), vmem(R // 4, 128),
             vmem(2, 3, 8, C), vmem(2, 2, 8, C), vmem(2, 2, R // 4, 128), vmem(2, 4, 8, 128),
             vmem(3, R, C), vmem(3, R, C), vmem(3, R, C), vmem(3, 8, C), vmem(R // 4, 128),
-            pltpu.SemaphoreType.DMA((6,)), pltpu.SemaphoreType.DMA((2, 8)), pltpu.SemaphoreType.DMA((2, 8)),
-            pltpu.SemaphoreType.DMA((5,)), pltpu.SemaphoreType.DMA((5,)), pltpu.SemaphoreType.REGULAR,
-            pltpu.SemaphoreType.REGULAR,
+            pltpu.SemaphoreType.DMA((7,)), pltpu.SemaphoreType.DMA((2, 8)), pltpu.SemaphoreType.DMA((2, 8)),
+            pltpu.SemaphoreType.DMA((8,)), pltpu.SemaphoreType.DMA((8,)), pltpu.SemaphoreType.DMA((8,)), pltpu.SemaphoreType.DMA((8,)),
+            pltpu.SemaphoreType.REGULAR, pltpu.SemaphoreType.REGULAR,
+            vmem(2, 3, 8, C), vmem(2, R // 4, 128), vmem(4, 8, 128), vmem(3, R, C), vmem(2, R, C), vmem(3, 1, 3),
+            pltpu.SMEM((3, 1, 3), F32), vmem(3, *ext), vmem(4, *ext),
         ],
         compiler_params=pltpu.CompilerParams(
             collective_id=0, has_side_effects=True, vmem_limit_bytes=32 * 1024 * 1024

time: 38.9 us -> 36.2 us (0.931)
  the two profiles are of different devices: /device:TPU:2 before, /device:TPU:31 now
where the time goes in v3:
time: 36.2 us; the launch traced here: 36.1 us
  Pallas kernels  35.4 us (98%)
  local copies, waits for them, and re-layouts  0.68 us (2%)
    pallas_call x1, Pallas kernels, per_device(): pl.pallas_call(functools.partial(kernel, sizes), out_shape=jax.ShapeDtype...  35.4 us

profile of v3, /device:TPU:31, one launch (start us, length us, event | category | flops | bytes accessed | tf_op | source)
XLA Modules:
  0.0 36.1 jit_solution(13353239099065909646)
XLA Ops:
  0.0 35.4 %window_product.1 = f32[1,3,64,256]{3,2,1,0:T(8,128)S(1)} custom-call(f32[1,3,64,256]{3,2,1,0:T(8,128)} %inc_h.1, f32[1,3,64,256]{3,2,1,0:T(8,128)} %mw_h.1, f32[1,2,64,256]{3,2,1,0:T(8,128)} %winds_h.1, f32[3,1,3]{2,1,0:T(1,128)} %bitcast.1, s32[1,1,1,1024]{3,2,1,0:T(1,128)} %cells_h.1, f32[1,3,1,1,1024]{4,3,2,1,0:T(1,128)} %ow_h.1), custom_call_target="tpu_custom_call" | custom-call | flops 10000000 | bytes 1000000 | tf_op jit(solution)/shard_map/window_product/pallas_call | solution.py:611
  35.4 0.7 %copy.8 = f32[1,3,64,256]{3,2,1,0:T(8,128)} copy(f32[1,3,64,256]{3,2,1,0:T(8,128)S(1)} %window_product.1) | data formatting | bytes 393216

commit v4 on v3

--- a/solution.py
+++ b/solution.py
@@ -131,18 +131,6 @@
             later = later | (lon == 0)
         return jnp.where(urgent, 0, jnp.where(later, 2, 1))
 
-    tile = (slice(None), pl.ds(0, R), pl.ds(0, C))
-    loads = [
-        pltpu.make_async_copy(cells_h.at[0, 0], cells_v, load_sem.at[0]),
-        pltpu.make_async_copy(ow_h.at[0, :, 0], ow_v, load_sem.at[1]),
-        pltpu.make_async_copy(inc_h.at[0], x_ext.at[tile], load_sem.at[2]),
-        pltpu.make_async_copy(winds_h.at[0], u_ext.at[tile], load_sem.at[3]),
-        pltpu.make_async_copy(mw_h.at[0], mw_v, load_sem.at[4]),
-        pltpu.make_async_copy(rea_h, rea_s, load_sem.at[5]),
-    ]
-    for load in loads:
-        load.start()
-
     barrier = pltpu.get_barrier_semaphore()
 
     def tell(ok, target):
@@ -150,12 +138,20 @@
         def _():
             pl.semaphore_signal(barrier, inc=1, device_id=target, device_id_type=MESH)
 
+    def is_near(d):
+        dlat, dlon = DIRS[d]
+        cut = lat < 0
+        if dlat:
+            cut = cut | (lat == (mid if dlat == 1 else mid - 1))
+        if dlon:
+            cut = cut | (lon == (0 if dlon == 1 else n_lon - 1))
+        return jnp.logical_not(cut)
+
     for d, (dlat, dlon) in enumerate(DIRS):
         for dw in range(2):
             source = (win + dw, lat - dlat, lon_at(-dlon))
             ok = lat_ok(-dlat) & jnp.logical_not(deferred(*source, d, dw) | answered(*source, d))
-            tell(ok & has_next if dw else ok, source)
-        tell(has_prev & lat_ok(dlat) & answered(win, lat, lon, d), (win - 1, lat + dlat, lon_at(dlon)))
+            tell((ok & has_next if dw else ok) & is_near(d), source)
     origin = (win == 0) & (lat == 0) & (lon == 0)
     follower = (win == 1) & (lat == 0) & (lon == 0)
     feeds = {
@@ -170,6 +166,25 @@
     tell(has_next, (win + 1, lat, lon))
     tell(has_prev, (win - 1, lat, lon))
 
+    tile = (slice(None), pl.ds(0, R), pl.ds(0, C))
+    loads = [
+        pltpu.make_async_copy(cells_h.at[0, 0], cells_v, load_sem.at[0]),
+        pltpu.make_async_copy(ow_h.at[0, :, 0], ow_v, load_sem.at[1]),
+        pltpu.make_async_copy(inc_h.at[0], x_ext.at[tile], load_sem.at[2]),
+        pltpu.make_async_copy(winds_h.at[0], u_ext.at[tile], load_sem.at[3]),
+        pltpu.make_async_copy(mw_h.at[0], mw_v, load_sem.at[4]),
+        pltpu.make_async_copy(rea_h, rea_s, load_sem.at[5]),
+    ]
+    for load in loads:
+        load.start()
+
+    for d, (dlat, dlon) in enumerate(DIRS):
+        for dw in range(2):
+            source = (win + dw, lat - dlat, lon_at(-dlon))
+            ok = lat_ok(-dlat) & jnp.logical_not(deferred(*source, d, dw) | answered(*source, d))
+            tell((ok & has_next if dw else ok) & jnp.logical_not(is_near(d)), source)
+        tell(has_prev & lat_ok(dlat) & answered(win, lat, lon, d), (win - 1, lat + dlat, lon_at(dlon)))
+
     for d, (dlat, dlon) in enumerate(DIRS):
         for dw in range(2):
             there = lat_ok(-dlat) & (has_next if dw else (win >= 0))
@@ -225,24 +240,6 @@
     for load in loads[2:]:
         load.wait()
     mix = [[rea_s[f, 0, g] + (KEEP if f == g else 0.0) for g in range(3)] for f in range(3)]
-
-    lane = iota((R, 128), 1)
-    packed = jnp.zeros((R, 128), F32)
-    own = [(x_ext, 0), (x_ext, 1), (x_ext, 2), (u_ext, 0), (u_ext, 1), (w_ext, 0), (w_ext, 1), (w_ext, 2), (mw_v, 0), (mw_v, 1), (mw_v, 2), (x_ext, 0), (x_ext, 1), (x_ext, 2)]
-    for a, (ref, f) in enumerate(own):
-        ends = jnp.where(lane < 64, ref[f, 0:R, 0:128], ref[f, 0:R, C - 128 : C])
-        packed = jnp.where((lane >= 8 * a) & (lane < 8 * a + 8), rolled(ends, 8 * a + 4, 1), packed)
-    pack[...] = packed
-    half = R // 2
-    low_lane = lax.rem(iota((half, 128), 1), 8) < 4
-    left = iota((half // 2, 128), 1) < 64
-    for e, pair in enumerate((
-        jnp.where(low_lane, packed[:half], rolled(packed[half:], 4, 1)),
-        jnp.where(low_lane, rolled(packed[half:], -4, 1), packed[:half]),
-    )):
-        upper, lower = pair[: half // 2], pair[half // 2 :]
-        cols[0, e] = jnp.where(left, upper, rolled(lower, 64, 1))
-        cols[1, e] = jnp.where(left, rolled(upper, 64, 1), lower)
 
     sub = iota((8, C), 0)
     lu, lv = u_ext[0, R - 8 : R, 0:C], u_ext[1, R - 8 : R, 0:C]
@@ -267,6 +264,24 @@
         rows_far[0, pair] = n_rows
         rows_far[1, pair] = n_cols
 
+    lane = iota((R, 128), 1)
+    packed = jnp.zeros((R, 128), F32)
+    own = [(x_ext, 0), (x_ext, 1), (x_ext, 2), (u_ext, 0), (u_ext, 1), (w_ext, 0), (w_ext, 1), (w_ext, 2), (mw_v, 0), (mw_v, 1), (mw_v, 2), (x_ext, 0), (x_ext, 1), (x_ext, 2)]
+    for a, (ref, f) in enumerate(own):
+        ends = jnp.where(lane < 64, ref[f, 0:R, 0:128], ref[f, 0:R, C - 128 : C])
+        packed = jnp.where((lane >= 8 * a) & (lane < 8 * a + 8), rolled(ends, 8 * a + 4, 1), packed)
+    pack[...] = packed
+    half = R // 2
+    low_lane = lax.rem(iota((half, 128), 1), 8) < 4
+    left = iota((half // 2, 128), 1) < 64
+    for e, pair in enumerate((
+        jnp.where(low_lane, packed[:half], rolled(packed[half:], 4, 1)),
+        jnp.where(low_lane, rolled(packed[half:], -4, 1), packed[:half]),
+    )):
+        upper, lower = pair[: half // 2], pair[half // 2 :]
+        cols[0, e] = jnp.where(left, upper, rolled(lower, 64, 1))
+        cols[1, e] = jnp.where(left, rolled(upper, 64, 1), lower)
+
     lats = 1 + lat_ok(1).astype(jnp.int32) + lat_ok(-1).astype(jnp.int32)
     prev, nxt = has_prev.astype(jnp.int32), has_next.astype(jnp.int32)
     ends = (is_last(lat, lon) | is_first(lat, lon)).astype(jnp.int32)
@@ -429,6 +444,15 @@
             @pl.when(ok)
             def _(d=d, dw=dw):
                 message(d, dw).wait_recv()
+
+    @pl.when(has_next)
+    def _():
+        bulk[0].wait_recv()
+        bulk[1].wait_recv()
+
+    for f in range(3):
+        g_ext[f, 0:R, 0:C] = w_ext[f, 0:R, 0:C] + mw_n[f]
+        h_ext[f, 0:R, 0:C] = mw_n[f] * inc_n[f]
 
     arrive(0)
 
@@ -471,10 +495,6 @@
             c[2 * i + 1, R:E, C:] = jnp.where(inside[:, 0:128], more[R:E], 0.0)
 
     unpack(got_rows_own, own_cols, x_ext, coef)
-    for f in range(3):
-        w_ext[f, :, C:] = side(own_cols, 5 + f)
-        w_ext[f, R:E, 0:C] = rolled(jnp.where(sub < 4, got_rows_own[0, f], got_rows_own[1, f]), 4, 0)
-
     c_all = [coef[i] for i in range(4)]
     state = tangent([x_ext[f] for f in range(3)], c_all, mix)
     for f in range(3):
@@ -484,9 +504,11 @@
     ring = jnp.zeros((R, 128), F32)
     for f in range(3):
         t_ext[f] = state[f]
-        ring_r[f] = jnp.where(sub < 4, t_ext[f, 0:8, 0:C], t_ext[f, R - 8 : R, 0:C])
         ends = jnp.where(lane < 64, t_ext[f, 0:R, 0:128], t_ext[f, 0:R, C - 128 : C])
         ring = jnp.where((lane >= 8 * f) & (lane < 8 * f + 8), rolled(ends, 8 * f + 4, 1), ring)
+    edges = [jnp.where(sub < 4, t_ext[f, 0:8, 0:C], t_ext[f, R - 8 : R, 0:C]) for f in range(3)]
+    ring_r[0] = jnp.where((sub < 2) | (sub >= 6), edges[0], rolled(edges[1], 4, 0))
+    ring_r[1] = edges[2]
     quarter = R // 4
     folded = ring[0:quarter]
     group = iota((quarter, 128), 1)
@@ -499,13 +521,12 @@
         late[0].start()
         late[1].start()
 
+    for f in range(3):
+        w_ext[f, :, C:] = side(own_cols, 5 + f)
+        w_ext[f, R:E, 0:C] = rolled(jnp.where(sub < 4, got_rows_own[0, f], got_rows_own[1, f]), 4, 0)
+
     arrive(1)
     far_cols = columns(got_cols.at[1], got_corner.at[1], True)
-
-    @pl.when(has_next)
-    def _():
-        bulk[0].wait_recv()
-        bulk[1].wait_recv()
 
     for f in range(3):
         t, base = f // 2, 4 * (f % 2)
@@ -513,8 +534,6 @@
         inc_rows = jnp.where(sub < 4, rolled(north_rows, -base, 0), rolled(south_rows, base, 0))
         mw_rows = jnp.where(sub < 4, rolled(north_rows, -base - 2, 0), rolled(south_rows, base + 2, 0))
         mw_cols = side(far_cols, f)
-        g_ext[f, 0:R, 0:C] = w_ext[f, 0:R, 0:C] + mw_n[f]
-        h_ext[f, 0:R, 0:C] = mw_n[f] * inc_n[f]
         g_ext[f, R:E, 0:C] = w_ext[f, R:E, 0:C] + mw_rows
         h_ext[f, R:E, 0:C] = mw_rows * inc_rows
         g_ext[f, :, C:] = w_ext[f, :, C:] + mw_cols
@@ -526,7 +545,7 @@
         h_ext[f] = state[f]
     state = adjoint([h_ext[f] for f in range(3)], c_all, mix)
     for f in range(3):
-        h_ext[f] = state[f]
+        h_ext[f, 0:R, 0:C] = state[f][0:R, 0:C]
 
     @pl.when(follower)
     def _():
@@ -560,7 +579,7 @@
         folded = got_ring_c[...]
         ring = jnp.concatenate([rolled(folded, -32 * q, 1) for q in range(4)], axis=0)
         for f in range(3):
-            rows = got_ring_r[f]
+            rows = rolled(got_ring_r[f // 2], 4 * (f % 2), 0)
             got_fwd[f, 0:8] = jnp.where(sub < 2, rows, got_fwd[f, 0:8])
             got_fwd[f, R - 8 : R] = jnp.where(sub >= 6, rows, got_fwd[f, R - 8 : R])
             ends = rolled(ring, -8 * f - 4, 1)
@@ -617,9 +636,9 @@
             vmem(3, *ext), vmem(2, *ext), vmem(3, *ext), vmem(4, *ext), vmem(3, *ext), vmem(3, *ext), vmem(3, *ext),
             vmem(3, R, C), pltpu.SMEM((3, 1, 3), F32), pltpu.VMEM((1, count), jnp.int32), vmem(3, 1, count),
             vmem(R, 128), vmem(2, 2, R // 4, 128), vmem(2, 3, 8, C), vmem(2, 2, 8, C),
-            vmem(3, R, C), vmem(3, 8, C), vmem(R // 4, 128),
+            vmem(3, R, C), vmem(2, 8, C), vmem(R // 4, 128),
             vmem(2, 3, 8, C), vmem(2, 2, 8, C), vmem(2, 2, R // 4, 128), vmem(2, 4, 8, 128),
-            vmem(3, R, C), vmem(3, R, C), vmem(3, R, C), vmem(3, 8, C), vmem(R // 4, 128),
+            vmem(3, R, C), vmem(3, R, C), vmem(3, R, C), vmem(2, 8, C), vmem(R // 4, 128),
             pltpu.SemaphoreType.DMA((7,)), pltpu.SemaphoreType.DMA((2, 8)), pltpu.SemaphoreType.DMA((2, 8)),
             pltpu.SemaphoreType.DMA((8,)), pltpu.SemaphoreType.DMA((8,)), pltpu.SemaphoreType.DMA((8,)), pltpu.SemaphoreType.DMA((8,)),
             pltpu.SemaphoreType.REGULAR, pltpu.SemaphoreType.REGULAR,

time: 36.2 us -> 36.4 us (level)
  no operation moved by 1% of the time
where the time goes in v4:
time: 36.4 us; the launch traced here: 36.2 us
  Pallas kernels  35.5 us (98%)
  local copies, waits for them, and re-layouts  0.68 us (2%)
    pallas_call x1, Pallas kernels, per_device(): pl.pallas_call(functools.partial(kernel, sizes), out_shape=jax.ShapeDtype...  35.5 us

profile of v4, /device:TPU:31, one launch (start us, length us, event | category | flops | bytes accessed | tf_op | source)
XLA Modules:
  0.0 36.2 jit_solution(7495011741501113434)
XLA Ops:
  0.0 35.5 %window_product.1 = f32[1,3,64,256]{3,2,1,0:T(8,128)S(1)} custom-call(f32[1,3,64,256]{3,2,1,0:T(8,128)} %inc_h.1, f32[1,3,64,256]{3,2,1,0:T(8,128)} %mw_h.1, f32[1,2,64,256]{3,2,1,0:T(8,128)} %winds_h.1, f32[3,1,3]{2,1,0:T(1,128)} %bitcast.1, s32[1,1,1,1024]{3,2,1,0:T(1,128)} %cells_h.1, f32[1,3,1,1,1024]{4,3,2,1,0:T(1,128)} %ow_h.1), custom_call_target="tpu_custom_call" | custom-call | flops 10000000 | bytes 1000000 | tf_op jit(solution)/shard_map/window_product/pallas_call | solution.py:630
  35.5 0.7 %copy.8 = f32[1,3,64,256]{3,2,1,0:T(8,128)} copy(f32[1,3,64,256]{3,2,1,0:T(8,128)S(1)} %window_product.1) | data formatting | bytes 393216

commit v5 on v3

--- a/solution.py
+++ b/solution.py
@@ -226,24 +226,6 @@
         load.wait()
     mix = [[rea_s[f, 0, g] + (KEEP if f == g else 0.0) for g in range(3)] for f in range(3)]
 
-    lane = iota((R, 128), 1)
-    packed = jnp.zeros((R, 128), F32)
-    own = [(x_ext, 0), (x_ext, 1), (x_ext, 2), (u_ext, 0), (u_ext, 1), (w_ext, 0), (w_ext, 1), (w_ext, 2), (mw_v, 0), (mw_v, 1), (mw_v, 2), (x_ext, 0), (x_ext, 1), (x_ext, 2)]
-    for a, (ref, f) in enumerate(own):
-        ends = jnp.where(lane < 64, ref[f, 0:R, 0:128], ref[f, 0:R, C - 128 : C])
-        packed = jnp.where((lane >= 8 * a) & (lane < 8 * a + 8), rolled(ends, 8 * a + 4, 1), packed)
-    pack[...] = packed
-    half = R // 2
-    low_lane = lax.rem(iota((half, 128), 1), 8) < 4
-    left = iota((half // 2, 128), 1) < 64
-    for e, pair in enumerate((
-        jnp.where(low_lane, packed[:half], rolled(packed[half:], 4, 1)),
-        jnp.where(low_lane, rolled(packed[half:], -4, 1), packed[:half]),
-    )):
-        upper, lower = pair[: half // 2], pair[half // 2 :]
-        cols[0, e] = jnp.where(left, upper, rolled(lower, 64, 1))
-        cols[1, e] = jnp.where(left, rolled(upper, 64, 1), lower)
-
     sub = iota((8, C), 0)
     lu, lv = u_ext[0, R - 8 : R, 0:C], u_ext[1, R - 8 : R, 0:C]
     fu, fv = u_ext[0, 0:8, 0:C], u_ext[1, 0:8, 0:C]
@@ -266,6 +248,24 @@
             n_cols = bottom if n_cols is None else jnp.where(sub >= 4, bottom, n_cols)
         rows_far[0, pair] = n_rows
         rows_far[1, pair] = n_cols
+
+    lane = iota((R, 128), 1)
+    packed = jnp.zeros((R, 128), F32)
+    own = [(x_ext, 0), (x_ext, 1), (x_ext, 2), (u_ext, 0), (u_ext, 1), (w_ext, 0), (w_ext, 1), (w_ext, 2), (mw_v, 0), (mw_v, 1), (mw_v, 2), (x_ext, 0), (x_ext, 1), (x_ext, 2)]
+    for a, (ref, f) in enumerate(own):
+        ends = jnp.where(lane < 64, ref[f, 0:R, 0:128], ref[f, 0:R, C - 128 : C])
+        packed = jnp.where((lane >= 8 * a) & (lane < 8 * a + 8), rolled(ends, 8 * a + 4, 1), packed)
+    pack[...] = packed
+    half = R // 2
+    low_lane = lax.rem(iota((half, 128), 1), 8) < 4
+    left = iota((half // 2, 128), 1) < 64
+    for e, pair in enumerate((
+        jnp.where(low_lane, packed[:half], rolled(packed[half:], 4, 1)),
+        jnp.where(low_lane, rolled(packed[half:], -4, 1), packed[:half]),
+    )):
+        upper, lower = pair[: half // 2], pair[half // 2 :]
+        cols[0, e] = jnp.where(left, upper, rolled(lower, 64, 1))
+        cols[1, e] = jnp.where(left, rolled(upper, 64, 1), lower)
 
     lats = 1 + lat_ok(1).astype(jnp.int32) + lat_ok(-1).astype(jnp.int32)
     prev, nxt = has_prev.astype(jnp.int32), has_next.astype(jnp.int32)

time: 36.2 us -> 36.2 us (level)
  no operation moved by 1% of the time
where the time goes in v5:
time: 36.2 us; the launch traced here: 36.1 us
  Pallas kernels  35.4 us (98%)
  local copies, waits for them, and re-layouts  0.68 us (2%)
    pallas_call x1, Pallas kernels, per_device(): pl.pallas_call(functools.partial(kernel, sizes), out_shape=jax.ShapeDtype...  35.4 us

profile of v5, /device:TPU:31, one launch (start us, length us, event | category | flops | bytes accessed | tf_op | source)
XLA Modules:
  0.0 36.1 jit_solution(13353239099065909646)
XLA Ops:
  0.0 35.4 %window_product.1 = f32[1,3,64,256]{3,2,1,0:T(8,128)S(1)} custom-call(f32[1,3,64,256]{3,2,1,0:T(8,128)} %inc_h.1, f32[1,3,64,256]{3,2,1,0:T(8,128)} %mw_h.1, f32[1,2,64,256]{3,2,1,0:T(8,128)} %winds_h.1, f32[3,1,3]{2,1,0:T(1,128)} %bitcast.1, s32[1,1,1,1024]{3,2,1,0:T(1,128)} %cells_h.1, f32[1,3,1,1,1024]{4,3,2,1,0:T(1,128)} %ow_h.1), custom_call_target="tpu_custom_call" | custom-call | flops 10000000 | bytes 1000000 | tf_op jit(solution)/shard_map/window_product/pallas_call | solution.py:611
  35.4 0.7 %copy.8 = f32[1,3,64,256]{3,2,1,0:T(8,128)} copy(f32[1,3,64,256]{3,2,1,0:T(8,128)S(1)} %window_product.1) | data formatting | bytes 393216
